TPU v7x, 128 devices: a whole 4x4x4 slice. The times are simulated.
128 devices in a mesh: ctx: 8 (over x, z_lo), tp: 16 (over z_hi, y, core).
Axes of the slice: x: 4, y: 4, z: 4 (z_hi: 2, z_lo: 2; z = z_hi * 2 + z_lo), core: 2. Of those that a mesh axis runs over, the one named last changes fastest.
Arguments:
- queries: bfloat16 [8192, 2048], P('ctx', 'tp'), may hold values from -6 to 6
- keys: bfloat16 [8192, 128], P(('ctx', 'tp')), may hold values from -6 to 6
- values: bfloat16 [8192, 128], P(('ctx', 'tp')), may hold values from -6 to 6
- outputs: bfloat16 [8192, 2048], P('ctx', 'tp'), may hold values from -6 to 6
- out_grad: bfloat16 [8192, 2048], P('ctx', 'tp'), may hold values from -6 to 6
- log_norm: float32 [16, 8192], P('tp', 'ctx'), may hold values from 4 to 6
- doc_ids: int32 [8192], replicated, may hold values from 0 to 7, never falling along the last dimension, each value on 1 to 5120 neighbouring positions
Outputs:
- query_grad: bfloat16 [8192, 2048], P('ctx', 'tp')
- key_grad: bfloat16 [8192, 128], P(('ctx', 'tp'))
- value_grad: bfloat16 [8192, 128], P(('ctx', 'tp'))
Inputs may be any that keep to these rules, and one draw needn't show every extreme that they name: `doc_ids`: document numbers never fall along the positions; each document has 1 to 5120 positions, one exactly that many.
All inputs are finite; a program needn't handle non-finite values.
Results may differ from a plain program's by a relative error of at most 0.006.
Values may be sent and summed in bfloat16 or wider, within the bound.
A program may use at most 64 MiB of HBM per device.

v0:
```python
import jax
import jax.numpy as jnp
from jax import lax
from jax.sharding import PartitionSpec as P


def body(queries, keys, values, outputs, out_grad, log_norm, doc_ids):
    rows = queries.shape[0]
    head_dim = keys.shape[1]
    scale = float(head_dim) ** (-0.5)
    n_ctx = lax.axis_size("ctx")
    my_ctx = lax.axis_index("ctx")
    sections = ((my_ctx * rows, 0, rows),)
    lse_all = log_norm[0]
    delta_all = jnp.sum(out_grad.astype(jnp.float32) * outputs.astype(jnp.float32), axis=-1)

    def tile(key_blk, value_blk, k_start, p_first, length):
        width = key_blk.shape[0]
        q_pos = p_first + jnp.arange(length, dtype=jnp.int32)
        q_doc = lax.dynamic_slice_in_dim(doc_ids, p_first, length)
        k_pos = k_start + jnp.arange(width, dtype=jnp.int32)
        k_doc = lax.dynamic_slice_in_dim(doc_ids, k_start, width)
        allowed = (k_pos[None, :] <= q_pos[:, None]) & (k_doc[None, :] == q_doc[:, None])
        scores = jnp.dot(queries, key_blk.T, preferred_element_type=jnp.float32) * scale
        prob = jnp.where(allowed, jnp.exp(scores - lse_all[:, None]), jnp.float32(0.0))
        prob_low = prob.astype(jnp.bfloat16)
        dprob = jnp.dot(out_grad, value_blk.T, preferred_element_type=jnp.float32)
        dscore = (prob * (dprob - delta_all[:, None])).astype(jnp.bfloat16)
        dims = (((0,), (0,)), ((), ()))
        q_part = jnp.dot(dscore, key_blk, preferred_element_type=jnp.float32)
        k_part = lax.dot_general(dscore, queries, dims, preferred_element_type=jnp.float32) * scale
        v_part = lax.dot_general(prob_low, out_grad, dims, preferred_element_type=jnp.float32)
        return (q_part, k_part, v_part)

    q_zero = jnp.zeros((rows, head_dim), jnp.float32)
    key_blk, value_blk = (
        lax.all_gather(keys, "tp", axis=0, tiled=True),
        lax.all_gather(values, "tp", axis=0, tiled=True),
    )
    total = rows * n_ctx
    full_zero = jnp.zeros((total, head_dim), jnp.float32)
    key_rows = lax.all_gather(key_blk, "ctx", axis=0, tiled=True)
    value_rows = lax.all_gather(value_blk, "ctx", axis=0, tiled=True)
    count = key_rows.shape[0]
    block = 512

    def one_block(step, inner):
        q_acc, k_acc, v_acc = inner
        offset = step * block
        key_blk = lax.dynamic_slice_in_dim(key_rows, offset, block)
        value_blk = lax.dynamic_slice_in_dim(value_rows, offset, block)
        p_first, row_off, length = sections[0]
        q_part, k_part, v_part = tile(key_blk, value_blk, offset, p_first, length)
        q_pieces = [q_part]
        k_old = lax.dynamic_slice_in_dim(k_acc, offset, block)
        v_old = lax.dynamic_slice_in_dim(v_acc, offset, block)
        k_acc = lax.dynamic_update_slice_in_dim(k_acc, k_old + k_part, offset, 0)
        v_acc = lax.dynamic_update_slice_in_dim(v_acc, v_old + v_part, offset, 0)
        return (q_acc + jnp.concatenate(q_pieces, axis=0), k_acc, v_acc)

    q_acc, k_full, v_full = lax.fori_loop(
        0, count // block, one_block, (q_zero, full_zero, full_zero)
    )
    key_sum, value_sum = (
        lax.psum_scatter(k_full, ("ctx", "tp"), scatter_dimension=0, tiled=True),
        lax.psum_scatter(v_full, ("ctx", "tp"), scatter_dimension=0, tiled=True),
    )
    query_grad = (q_acc * scale).astype(jnp.bfloat16)
    return (query_grad, key_sum.astype(jnp.bfloat16), value_sum.astype(jnp.bfloat16))


def solution(mesh):
    return jax.shard_map(
        body,
        mesh=mesh,
        in_specs=(
            P("ctx", "tp"),
            P(("ctx", "tp"), None),
            P(("ctx", "tp"), None),
            P("ctx", "tp"),
            P("ctx", "tp"),
            P("tp", "ctx"),
            P(),
        ),
        out_specs=(P("ctx", "tp"), P(("ctx", "tp"), None), P(("ctx", "tp"), None)),
        check_vma=False,
    )
```

profile of v0, /device:TPU:0, one launch (start us, length us, event | category | flops | bytes accessed | tf_op | source)
XLA Modules:
  0.0 1587.0 jit_solution(12240125341256198215)
XLA Ops:
  7.2 27.7 %all_gather.12 = bf16[1024,128]{1,0:T(8,128)(2,1)} all-gather(bf16[64,128]{1,0:T(8,128)(2,1)} %param.10), channel_id=1, replica_groups=mesh['ctx'=8,'tp'=16] {'tp'}, dimensions={0}, use_global_device_ids=true | all-gather | bytes 278528 | tf_op jit(solution)/shard_map/all_gather | solution.py:37
  35.0 22.0 %all_gather.14 = bf16[1024,128]{1,0:T(8,128)(2,1)} all-gather(bf16[64,128]{1,0:T(8,128)(2,1)} %param.11), channel_id=1, replica_groups=mesh['ctx'=8,'tp'=16] {'tp'}, dimensions={0}, use_global_device_ids=true | all-gather | bytes 278528 | tf_op jit(solution)/shard_map/all_gather | solution.py:38
  59.0 24.8 %all-gather.3.cloned.1.call-done = bf16[8192,128]{1,0:T(8,128)(2,1)} async-done(((bf16[1024,128]{1,0:T(8,128)(2,1)}), bf16[8192,128]{1,0:T(8,128)(2,1)}) %all-gather.3.cloned.1.call-update) | async-done | bytes 2097168 | tf_op jit(solution)/shard_map/all_gather | solution.py:42
  83.8 54.0 %all-gather.5.cloned.1.call-done = bf16[8192,128]{1,0:T(8,128)(2,1)} async-done(((bf16[1024,128]{1,0:T(8,128)(2,1)}), bf16[8192,128]{1,0:T(8,128)(2,1)}) %all-gather.5.cloned.1.call-update) | async-done | bytes 2097168 | tf_op jit(solution)/shard_map/all_gather | solution.py:43
  137.8 2.3 broadcast_in_dim.32.clone
  140.1 2.2 broadcast_in_dim.32
  142.3 151.5 %while.20 = (s32[]{:T(128)}, f32[1024,128]{1,0:T(8,128)S(1)}, f32[8192,128]{1,0:T(8,128)}, f32[8192,128]{1,0:T(8,128)}, s32[]{:T(128)}, /*index=5*/s32[8192]{0:T...) while((s32[]{:T(128)}, f32[1024,128]{1,0:T(8,128)S(1)}, ...), condition=%wide.region_2.3_spmd.clone, body=%wide.region_1.2_spmd.clone.sunk | while | flops 676791808 | bytes 13007101 | solution.py:61
  147.6 2.1 fusion.42
  149.7 2.1 fusion.41
  157.0 2.1 fusion.42
  159.2 2.1 fusion.41
  166.5 2.1 fusion.42
  176.0 2.1 fusion.42
  185.5 2.1 fusion.42
  187.6 2.1 fusion.41
  194.9 2.1 fusion.42
  204.4 2.1 fusion.42
  213.8 2.1 fusion.42
  215.9 2.1 fusion.41
  223.3 2.1 fusion.42
  232.7 2.1 fusion.42
  234.9 2.1 fusion.41
  242.2 2.1 fusion.42
  244.3 2.1 fusion.41
  251.7 2.1 fusion.42
  253.8 2.1 fusion.41
  261.2 2.1 fusion.42
  263.3 2.1 fusion.41
  280.1 2.1 fusion.42
  289.6 2.1 fusion.42
  295.1 643.7 %reduce-scatter.5.cloned.1.call-done = f32[64,128]{1,0:T(8,128)} async-done(((f32[8192,128]{1,0:T(8,128)}), f32[64,128]{1,0:T(8,128)}) %reduce-scatter.5.cloned.1.call-update) | async-done | bytes 32784 | tf_op jit(solution)/shard_map/reduce_scatter | solution.py:66
  940.2 639.0 %reduce-scatter.3.cloned.1.call-done = f32[64,128]{1,0:T(8,128)} async-done(((f32[8192,128]{1,0:T(8,128)}), f32[64,128]{1,0:T(8,128)}) %reduce-scatter.3.cloned.1.call-update) | async-done | bytes 32784 | tf_op jit(solution)/shard_map/reduce_scatter | solution.py:65
  (125 shorter events, 108.9 us)
Async XLA Ops:
  7.2 76.6 %all-gather.3.cloned.1.call-start = ((), (), s32[]{:S(2)}) async-start(), calls=%async_computation.2 | async-start | bytes 2359296 | tf_op jit(solution)/shard_map/all_gather | solution.py:42
  34.9 102.9 %all-gather.5.cloned.1.call-start = ((), (), s32[]{:S(2)}) async-start(), calls=%async_computation.3 | async-start | bytes 2359296 | tf_op jit(solution)/shard_map/all_gather | solution.py:43
  57.0 881.8 %reduce-scatter.5.cloned.1.call-start = ((), (), s32[]{:S(2)}) async-start(), calls=%async_computation.5 | async-start | bytes 4227072 | tf_op jit(solution)/shard_map/reduce_scatter | solution.py:66
  140.1 2.2 copy-start
  140.1 2.2 copy-start.1
  140.1 2.2 copy-start.2
  293.8 1285.3 %reduce-scatter.3.cloned.1.call-start = ((), (), s32[]{:S(2)}) async-start(), calls=%async_computation.4 | async-start | bytes 4227072 | tf_op jit(solution)/shard_map/reduce_scatter | solution.py:65
Sparse Core Ops, SparseCore 0:
  35.0 48.7 all-gather.2
  85.4 52.3 all-gather.4
  293.9 644.8 reduce-scatter.4
  941.1 637.9 reduce-scatter.2
where the time goes:
time: 1590 us
  waiting for transfers between devices  1360 us (86%)
  matrix products  139 us (9%)
  blocking collectives  49.7 us (3%)
  local copies, waits for them, and re-layouts  17.3 us (1%)
    reduce_scatter x1, waiting for transfers between devices, body(): lax.psum_scatter(v_full, ('ctx', 'tp'), scatter_dimension=0, tiled=True)  644 us
    reduce_scatter x1, waiting for transfers between devices, body(): lax.psum_scatter(k_full, ('ctx', 'tp'), scatter_dimension=0, tiled=True)  639 us
    all_gather x1, waiting for transfers between devices, body(): value_rows = lax.all_gather(value_blk, 'ctx', axis=0, tiled=True)  54 us
    dot_general x16, matrix products, tile(): lax.dot_general(prob_low, out_grad, dims, preferred_element_type=jnp.floa...  33.7 us
    dot_general x16, matrix products, tile(): lax.dot_general(dscore, queries, dims, preferred_element_type=jnp.float32)  33.4 us
  transfers between devices with their start and end apart: 4, of which 4 were waited for; matrix products, arithmetic and copies ran while one was open for 0% of the time, Pallas kernels for 0%

commit v1 on v0

v1 whole, which is shorter than its diff:
```python
import functools
import math

import jax
import jax.numpy as jnp
from jax import lax
from jax.experimental import pallas as pl
from jax.experimental.pallas import tpu as pltpu
from jax.sharding import PartitionSpec as P

MESH = pl.DeviceIdType.MESH
SPAN = 5120
FAR = 8192.0
F32 = jnp.float32
BF16 = jnp.bfloat16


def split3(x):
    hi = x.astype(BF16).astype(F32)
    mid = (x - hi).astype(BF16).astype(F32)
    return hi, mid, x - hi - mid


def dot(a, b):
    return jnp.dot(a, b, preferred_element_type=F32)


def kernel(
    n_ctx, n_tp, steps,
    q_in, k_in, v_in, o_in, g_in, lse_in, doc_in,
    dq_out, dk_out, dv_out,
    qn, gn, on, qt, gt, xt, kv, fk, kt, acc, dqt, dqs, part, rs, back, fin, tot,
    lse, doc, doc_a, doc_b,
    in_sem, sib_send, sib_recv, s1, r1, s2, r2, s3, r3, s4, r4,
):
    rows, hd = qn.shape[1], qn.shape[2]
    half = n_tp // 2
    own = rows // n_tp
    width = own * half
    lines = rows // 128
    scale = float(hd) ** -0.5
    c = lax.axis_index("ctx")
    t = lax.axis_index("tp")
    core = t % 2
    u = t // 2
    sib = (c, t + 1 - 2 * core)
    mine = pl.ds(pl.multiple_of(u * own, own), own)

    loads = [
        pltpu.make_async_copy(src, dst, in_sem.at[i])
        for i, (src, dst) in enumerate((
            (k_in, kv.at[0, 0, mine]), (v_in, kv.at[0, 1, mine]), (q_in, qn.at[0]), (g_in, gn.at[0]),
            (o_in, on), (lse_in, lse), (doc_in, doc),
        ))
    ]
    for load in loads:
        load.start()

    barrier = pltpu.get_barrier_semaphore()
    pl.semaphore_signal(barrier, inc=1, device_id=sib, device_id_type=MESH)

    def greet_tp(j, _):
        pl.semaphore_signal(barrier, inc=1, device_id=(c, ((u + j) % half) * 2 + core), device_id_type=MESH)
        return 0

    def greet_ctx(j, _):
        pl.semaphore_signal(barrier, inc=1, device_id=((c + j) % n_ctx, t), device_id_type=MESH)
        return 0

    lax.fori_loop(1, half, greet_tp, 0)
    lax.fori_loop(1, n_ctx, greet_ctx, 0)
    for load in loads[:4]:
        load.wait()
    pl.semaphore_wait(barrier, 1 + half - 1 + n_ctx - 1)

    def copy1(s):
        return pltpu.make_async_remote_copy(
            kv.at[0, :, mine], kv.at[s, :, mine], s1.at[s], r1.at[s], ((c + s) % n_ctx, t), MESH)

    def copy2(s, j):
        return pltpu.make_async_remote_copy(
            kv.at[s, :, mine], kv.at[s, :, mine], s2.at[s], r2.at[s], (c, ((u + j) % half) * 2 + core), MESH)

    def spread(s):
        def one(j, _):
            copy2(s, j).start()
            return 0
        lax.fori_loop(1, half, one, 0)

    def for_steps(first, last, fn):
        def one(s, _):
            fn(s)
            return 0
        lax.fori_loop(first, last, one, 0)

    def when_sends(fn):
        def run(s):
            @pl.when(c + s < n_ctx)
            def _():
                fn(s)
        return run

    def when_has(fn):
        def run(s):
            @pl.when(c >= s)
            def _():
                fn(s)
        return run

    for_steps(1, steps, when_sends(lambda s: copy1(s).start()))
    spread(0)
    sib_q = pltpu.make_async_remote_copy(qn.at[0], qn.at[1], sib_send.at[0], sib_recv.at[0], sib, MESH)
    sib_g = pltpu.make_async_remote_copy(gn.at[0], gn.at[1], sib_send.at[1], sib_recv.at[1], sib, MESH)
    sib_x = pltpu.make_async_remote_copy(
        xt.at[0, pl.ds(0, 16)], xt.at[1, pl.ds(0, 16)], sib_send.at[2], sib_recv.at[2], sib, MESH)
    sib_d = pltpu.make_async_remote_copy(dqt.at[1], dqs, sib_send.at[3], sib_recv.at[3], sib, MESH)
    sib_q.start()
    sib_g.start()

    for load in loads[4:]:
        load.wait()
    g_t = gn[0].T
    qt[0] = qn[0].T
    gt[0] = g_t
    delta = jnp.sum(g_t.astype(F32) * on[...].T.astype(F32), axis=0, keepdims=True)
    q_doc = jnp.concatenate([doc[pl.ds(c * lines + j, 1), :] for j in range(lines)], axis=1)
    place = lax.broadcasted_iota(jnp.int32, (8, rows), 0)
    extra = jnp.zeros((8, rows), F32)
    for i, row in enumerate((*split3(lse[...] * math.sqrt(hd)), *split3(delta))):
        extra = jnp.where(place == i, -row, extra)
    xt[0, 0:8, :] = jnp.where(place == q_doc, -FAR, 0.0).astype(BF16)
    xt[0, 8:16, :] = extra.astype(BF16)
    sib_x.start()
    for h in range(2):
        xt[h, 16:, :] = jnp.zeros((hd - 16, rows), BF16)

    for_steps(1, steps, when_has(lambda s: (copy1(s).wait_recv(), spread(s))))

    turned = pltpu.roll(doc[...], 64, 1)
    doc_a[...] = jnp.where(core == 0, doc[...], turned)
    doc_b[...] = jnp.where(core == 0, turned, doc[...])
    lane = lax.broadcasted_iota(jnp.int32, (128, 128), 1)

    def features(s):
        for m in range(lines // 2):
            at = (c - s) * lines + 2 * m
            both = jnp.where(lane < 64, doc_a[pl.ds(at, 1), :], doc_b[pl.ds(at + 1, 1), :])
            other = jnp.where((lane < 11) & (both.T != lane), 1.0, 0.0)
            fk[s, m * 128:(m + 1) * 128, :] = other.astype(BF16)

    for_steps(0, steps, when_has(features))

    v_lane = lax.broadcasted_iota(jnp.int32, (1, 128), 1)
    v_row = jnp.where((v_lane >= 11) & (v_lane < 14), 1.0, 0.0).astype(BF16)

    def arrive(s):
        got = kv.at[s, :, pl.ds(0, width - own)]
        pltpu.make_async_copy(got, got, r2.at[s]).wait()
        kt[...] = kv[s, 0].T
        acc[...] = jnp.zeros_like(acc)

    def tile(h, s, q0, tq, k0, tk, diagonal):
        qs, ks = pl.ds(q0, tq), pl.ds(k0, tk)
        x = xt[h, :, qs]
        k_all = jnp.concatenate([kv[s, 0, ks], fk[s, ks]], axis=1)
        v_all = jnp.concatenate([kv[s, 1, ks], jnp.broadcast_to(v_row, (tk, 128))], axis=1)
        prob = jnp.exp2(dot(k_all, jnp.concatenate([qt[h, :, qs], x], axis=0)) * (scale * math.log2(math.e)))
        if diagonal:
            r = k0 + lax.broadcasted_iota(jnp.int32, (tk, tq), 0)
            k_pos = (r // own * 2 + core) * own + r % own
            prob = jnp.where(k_pos <= q0 + lax.broadcasted_iota(jnp.int32, (tk, tq), 1), prob, 0.0)
        dprob = dot(v_all, jnp.concatenate([gt[h, :, qs], x], axis=0))
        low = prob.astype(BF16)
        dscore = (prob * dprob).astype(BF16)
        acc[0, ks] += dot(dscore, qn[h, qs])
        acc[1, ks] += dot(low, gn[h, qs])
        dqt[h, :, qs] += dot(kt[:, ks], dscore)

    def copy3(s, j):
        to = (u + j) % half
        rows_to = pl.ds(pl.multiple_of(to * own, own), own)
        return pltpu.make_async_remote_copy(
            part.at[s, :, rows_to], rs.at[s, j - 1], s3.at[s], r3.at[s], (c, to * 2 + core), MESH)

    def hand_out(s):
        part[s] = acc[...].astype(BF16)

        def one(j, _):
            copy3(s, j).start()
            return 0
        lax.fori_loop(1, half, one, 0)

    def gathered(s):
        pltpu.make_async_copy(rs.at[s], rs.at[s], r3.at[s]).wait()
        total = part[s, :, mine].astype(F32)
        for j in range(half - 1):
            total += rs[s, j].astype(F32)
        return total

    def copy4(s):
        return pltpu.make_async_remote_copy(
            back.at[s], fin.at[s], s4.at[s], r4.at[s], ((c + n_ctx - s) % n_ctx, t), MESH)

    def reduce(s):
        back[s] = gathered(s).astype(BF16)
        copy4(s).start()

    dqt[...] = jnp.zeros_like(dqt)
    tq = min(256, rows)

    arrive(0)

    def own_tiles(h):
        for q0 in range(0, rows, tq):
            tile(h, 0, q0, tq, 0, (q0 + tq) // 2, True)

    own_tiles(0)
    sib_q.wait_recv()
    sib_g.wait_recv()
    sib_x.wait_recv()
    qt[1] = qn[1].T
    gt[1] = gn[1].T
    own_tiles(1)
    hand_out(0)
    pl.when(c == 0)(lambda: sib_d.start())

    def step(s):
        def work():
            arrive(s)

            def two(i, _):
                h = 1 - i
                if isinstance(s, int) and s * rows == SPAN:
                    for q0 in range(0, rows, tq):
                        tile(h, s, q0, tq, q0 // 2, width - q0 // 2, False)
                else:
                    def over(n, _):
                        tile(h, s, pl.multiple_of(n * tq, tq), tq, 0, width, False)
                        return 0
                    lax.fori_loop(0, rows // tq, over, 0)

                @pl.when((i == 0) & ((c == s) | (s == steps - 1)))
                def _():
                    sib_d.start()
                return 0

            lax.fori_loop(0, 2, two, 0)
            hand_out(s)

        pl.when(c >= s)(work)

    last = steps - 1 if (steps - 1) * rows == SPAN else steps
    if last > 1:
        step(1)
        tot[...] = gathered(0)

    def middle(s):
        step(s)
        pl.when(c >= s - 1)(lambda: reduce(s - 1))

    for_steps(2, last, middle)
    if last < steps:
        middle(last)
    pl.when(c >= steps - 1)(lambda: reduce(steps - 1))

    sib_d.wait_recv()
    dq_out[...] = ((dqt[0] + dqs[...]) * scale).T.astype(BF16)

    def collect(s):
        copy4(s).wait_recv()
        tot[...] += fin[s].astype(F32)

    for_steps(1, steps, when_sends(collect))
    dk_out[...] = (tot[0] * scale).astype(BF16)
    dv_out[...] = tot[1].astype(BF16)

    sib_q.wait_send()
    sib_g.wait_send()
    sib_x.wait_send()
    sib_d.wait_send()

    def sent(s):
        out = kv.at[s, :, pl.ds(0, width - own)]
        pltpu.make_async_copy(out, out, s2.at[s]).wait()
        gone = part.at[s, :, pl.ds(0, width - own)]
        pltpu.make_async_copy(gone, gone, s3.at[s]).wait()

    for_steps(0, steps, when_has(sent))
    for_steps(1, steps, when_sends(lambda s: copy1(s).wait_send()))
    for_steps(1, steps, when_has(lambda s: copy4(s).wait_send()))


def body(n_ctx, n_tp, queries, keys, values, outputs, out_grad, log_norm, doc_ids):
    rows, hd = queries.shape
    own = keys.shape[0]
    half = n_tp // 2
    width = own * half
    steps = min(n_ctx, -(-SPAN // rows) + 1)
    doc_ids = doc_ids.reshape(-1, 128)
    dma = pltpu.SemaphoreType.DMA
    anywhere = pl.BlockSpec(memory_space=pl.ANY)
    inside = pl.BlockSpec(memory_space=pltpu.VMEM)
    return pl.pallas_call(
        functools.partial(kernel, n_ctx, n_tp, steps),
        out_shape=(
            jax.ShapeDtypeStruct((rows, hd), BF16),
            jax.ShapeDtypeStruct((own, hd), BF16),
            jax.ShapeDtypeStruct((own, hd), BF16),
        ),
        in_specs=[anywhere] * 7,
        out_specs=(inside, inside, inside),
        scratch_shapes=[
            pltpu.VMEM((2, rows, hd), BF16),
            pltpu.VMEM((2, rows, hd), BF16),
            pltpu.VMEM((rows, hd), BF16),
            pltpu.VMEM((2, hd, rows), BF16),
            pltpu.VMEM((2, hd, rows), BF16),
            pltpu.VMEM((2, hd, rows), BF16),
            pltpu.VMEM((steps, 2, width, hd), BF16),
            pltpu.VMEM((steps, width, hd), BF16),
            pltpu.VMEM((hd, width), BF16),
            pltpu.VMEM((2, width, hd), F32),
            pltpu.VMEM((2, hd, rows), F32),
            pltpu.VMEM((hd, rows), F32),
            pltpu.VMEM((steps, 2, width, hd), BF16),
            pltpu.VMEM((steps, half - 1, 2, own, hd), BF16),
            pltpu.VMEM((steps, 2, own, hd), BF16),
            pltpu.VMEM((steps, 2, own, hd), BF16),
            pltpu.VMEM((2, own, hd), F32),
            pltpu.VMEM((1, rows), F32),
            pltpu.VMEM(doc_ids.shape, jnp.int32),
            pltpu.VMEM(doc_ids.shape, jnp.int32),
            pltpu.VMEM(doc_ids.shape, jnp.int32),
            dma((7,)), dma((4,)), dma((4,)),
            *[dma((steps,)) for _ in range(8)],
        ],
        compiler_params=pltpu.CompilerParams(
            collective_id=0, has_side_effects=True, vmem_limit_bytes=48 * 1024 * 1024),
    )(queries, keys, values, outputs, out_grad, log_norm, doc_ids)


def solution(mesh):
    return jax.shard_map(
        functools.partial(body, mesh.shape["ctx"], mesh.shape["tp"]),
        mesh=mesh,
        in_specs=(
            P("ctx", "tp"),
            P(("ctx", "tp"), None),
            P(("ctx", "tp"), None),
            P("ctx", "tp"),
            P("ctx", "tp"),
            P("tp", "ctx"),
            P(),
        ),
        out_specs=(P("ctx", "tp"), P(("ctx", "tp"), None), P(("ctx", "tp"), None)),
        check_vma=False,
    )
```

time: 1590 us -> 75 us (0.05)
  waiting for transfers between devices: 1360 us -> 0 us
  matrix products: 139 us -> 0 us
  Pallas kernels: 0 us -> 66.3 us
  blocking collectives: 49.7 us -> 0 us
    reduce_scatter x2 -> x0, waiting for transfers between devices: 1280 us -> none  [the longest x1 644 us: body(): lax.psum_scatter(v_full, ('ctx', 'tp'), scatter_dimension=0, tiled=True)]
    dot_general x80 -> x0, matrix products: 139 us -> none  [the longest x16 33.7 us: tile(): lax.dot_general(prob_low, out_grad, dims, preferred_element_type=jnp.floa...]
    all_gather x2 -> x0, waiting for transfers between devices: 78.8 us -> none  [the longest x1 54 us: body(): value_rows = lax.all_gather(value_blk, 'ctx', axis=0, tiled=True)]
    pallas_call x0 -> x1, Pallas kernels: none -> 66.3 us  [body(): pl.pallas_call(functools.partial(kernel, n_ctx, n_tp, steps), out_shape=(...]
    all_gather x2 -> x0, blocking collectives: 49.7 us -> none  [the longest x1 27.7 us: body(): lax.all_gather(keys, 'tp', axis=0, tiled=True)]
  transfers between devices with their start and end apart: 4 -> 0, of which waited for: 4 -> 0; matrix products, arithmetic and copies ran while one was open for 0% -> 0% of each run, Pallas kernels for 0% -> 0%
where the time goes in v1:
time: 75 us; the launch traced here: 74.5 us
  Pallas kernels  66.3 us (88%)
  local copies, waits for them, and re-layouts  7.63 us (10%)
    pallas_call x1, Pallas kernels, body(): pl.pallas_call(functools.partial(kernel, n_ctx, n_tp, steps), out_shape=(...  66.3 us
    unnamed x17, local copies, waits for them, and re-layouts  7.63 us

profile of v1, /device:TPU:0, one launch (start us, length us, event | category | flops | bytes accessed | tf_op | source)
XLA Modules:
  0.0 74.5 jit_solution(14793258802246632042)
XLA Ops:
  0.6 0.0 copy-start
  0.6 0.9 %copy-done = bf16[1024,128]{1,0:T(8,128)(2,1)S(1)} copy-done((bf16[1024,128]{1,0:T(8,128)(2,1)S(1)}, bf16[1024,128]{1,0:T(8,128)(2,1)}, u32[]{:S(2)}) %copy-start) | copy-done | bytes 262168
  1.6 0.0 copy-start.1
  1.6 0.9 %copy-done.1 = bf16[1024,128]{1,0:T(8,128)(2,1)S(1)} copy-done((bf16[1024,128]{1,0:T(8,128)(2,1)S(1)}, bf16[1024,128]{1,0:T(8,128)(2,1)}, u32[]{:S(2)}) %copy-start.1) | copy-done | bytes 262168
  2.5 0.0 copy-start.2
  2.5 0.9 %copy-done.2 = bf16[1024,128]{1,0:T(8,128)(2,1)S(1)} copy-done((bf16[1024,128]{1,0:T(8,128)(2,1)S(1)}, bf16[1024,128]{1,0:T(8,128)(2,1)}, u32[]{:S(2)}) %copy-start.2) | copy-done | bytes 262168
  3.5 0.0 copy-start.3
  3.5 0.8 %copy-done.3 = s32[8192]{0:T(1024)S(1)} copy-done((s32[8192]{0:T(1024)S(1)}, s32[8192]{0:T(1024)}, u32[]{:S(2)}) %copy-start.3) | copy-done | bytes 32792
  4.2 0.0 copy-start.4
  4.2 0.7 copy-done.4
  5.0 0.0 copy-start.5
  5.0 0.7 copy-done.5
  5.7 0.0 copy-start.6
  5.7 0.7 copy-done.6
  6.4 66.3 %shard_map.94 = (bf16[1024,128]{1,0:T(8,128)(2,1)S(1)}, bf16[64,128]{1,0:T(8,128)(2,1)S(1)}, bf16[64,128]{1,0:T(8,128)(2,1)S(1)}) custom-call(bf16[1024,128]{1,0:T(8,128)(2,1)S(1)} %copy-done, bf16[64,128]{1,0:T(8,128)(2,1)S(1)} %copy-done.4, bf16[64,128]{1,0:T(8,128)(2,1)S(1)} %copy-done.5, bf16[1024,128]{1,0:T(8,128)(2,1)S(1)} %copy-done.1, ...), custom_call_target="tpu_custom_call" | custom-call | tf_op jit(solution)/shard_map/pallas_call | solution.py:303
  72.6 0.7 copy.13
  73.3 0.6 copy.14
  73.9 0.6 copy.15
Async XLA Ops:
  0.6 1.0 %copy-start = (bf16[1024,128]{1,0:T(8,128)(2,1)S(1)}, bf16[1024,128]{1,0:T(8,128)(2,1)}, u32[]{:S(2)}) copy-start(bf16[1024,128]{1,0:T(8,128)(2,1)} %q_in.1) | copy-start | bytes 786436
  1.6 0.9 %copy-start.1 = (bf16[1024,128]{1,0:T(8,128)(2,1)S(1)}, bf16[1024,128]{1,0:T(8,128)(2,1)}, u32[]{:S(2)}) copy-start(bf16[1024,128]{1,0:T(8,128)(2,1)} %o_in.1) | copy-start | bytes 786436
  2.5 0.9 %copy-start.2 = (bf16[1024,128]{1,0:T(8,128)(2,1)S(1)}, bf16[1024,128]{1,0:T(8,128)(2,1)}, u32[]{:S(2)}) copy-start(bf16[1024,128]{1,0:T(8,128)(2,1)} %g_in.1) | copy-start | bytes 786436
  3.5 0.8 %copy-start.3 = (s32[8192]{0:T(1024)S(1)}, s32[8192]{0:T(1024)}, u32[]{:S(2)}) copy-start(s32[8192]{0:T(1024)} %param.13) | copy-start | bytes 98308
  4.2 0.7 copy-start.4
  5.0 0.7 copy-start.5
  5.7 0.7 copy-start.6

commit v2 on v1

v2 whole, which is shorter than its diff:
```python
import functools
import math

import jax
import jax.numpy as jnp
from jax import lax
from jax.experimental import pallas as pl
from jax.experimental.pallas import tpu as pltpu
from jax.sharding import PartitionSpec as P

MESH = pl.DeviceIdType.MESH
SPAN = 5120
FAR = 8192.0
F32 = jnp.float32
BF16 = jnp.bfloat16


def split3(x):
    hi = x.astype(BF16).astype(F32)
    mid = (x - hi).astype(BF16).astype(F32)
    return hi, mid, x - hi - mid


def dot(a, b):
    return jnp.dot(a, b, preferred_element_type=F32)


def kernel(
    n_ctx, n_tp, steps,
    q_in, k_in, v_in, o_in, g_in, lse_in, doc_in,
    dq_out, dk_out, dv_out,
    qn, gn, on, qt, gt, xt, kb, vb, fk, acc, dqt, dqs,
    part_k, rs_k, y_out, y_own, z_in, back, fin_k, tot_k,
    part_v, fin_v, tot_v, out_v, rs_v,
    lse, doc, doc_a, doc_b,
    in_sem, sib_send, sib_recv, near_send, near_recv, last_send, last_recv,
    s_a, r_a, s_z, r_z, s_y, r_y, s_b, r_b, s_p, r_p, s_q, r_q, s_f, r_f, s_g, r_g,
):
    rows, hd = qn.shape[1], qn.shape[2]
    half = n_tp // 2
    ys = half // 2
    own = rows // n_tp
    width = own * half
    lines = rows // 128
    scale = float(hd) ** -0.5
    c = lax.axis_index("ctx")
    t = lax.axis_index("tp")
    core = t % 2
    u = t // 2
    y = u % ys
    z = u // ys
    sib = (c, t + 1 - 2 * core)
    over_z = (c, ((1 - z) * ys + y) * 2 + core)

    loads = [
        pltpu.make_async_copy(src, dst, in_sem.at[i])
        for i, (src, dst) in enumerate((
            (k_in, kb.at[0, z, y]), (v_in, vb.at[0, z, y]), (q_in, qn.at[0]), (g_in, gn.at[0]),
            (o_in, on), (lse_in, lse), (doc_in, doc),
        ))
    ]
    for load in loads:
        load.start()

    def loop(first, last, fn):
        def one(i, _):
            fn(i)
            return 0
        lax.fori_loop(first, last, one, 0)

    def when_sends(fn):
        def run(s):
            @pl.when(c + s < n_ctx)
            def _():
                fn(s)
        return run

    def when_has(fn):
        def run(s):
            @pl.when(c >= s)
            def _():
                fn(s)
        return run

    def remote(src, dst, send, recv, to):
        return pltpu.make_async_remote_copy(src, dst, send, recv, to, MESH)

    def await_bytes(ref, sem):
        pltpu.make_async_copy(ref, ref, sem).wait()

    def peer(j):
        v = (u + j) % half
        return v // ys, v % ys, (c, v * 2 + core)

    def y_peer(j):
        w = (y + j) % ys
        return w, (c, (z * ys + w) * 2 + core)

    barrier = pltpu.get_barrier_semaphore()

    def greet(to):
        pl.semaphore_signal(barrier, inc=1, device_id=to, device_id_type=MESH)

    greet(sib)
    loop(1, half, lambda j: greet(peer(j)[2]))
    loop(1, n_ctx, lambda j: greet(((c + j) % n_ctx, t)))
    for load in loads[:2]:
        load.wait()
    pl.semaphore_wait(barrier, 1 + half - 1 + n_ctx - 1)

    def near_k(j):
        return remote(kb.at[0, z, y], kb.at[0, z, y], near_send.at[0], near_recv.at[0], peer(j)[2])

    def near_v(j):
        return remote(vb.at[0, z, y], vb.at[0, z, y], near_send.at[1], near_recv.at[1], peer(j)[2])

    def along_ctx(s):
        return remote(kb.at[0, z, y], kb.at[s, z, y], s_a.at[s], r_a.at[s], ((c + s) % n_ctx, t))

    def across_z(s):
        return remote(kb.at[s, z, y], kb.at[s, z, y], s_z.at[s], r_z.at[s], over_z)

    def along_y(s, j):
        return remote(kb.at[s, :, y], kb.at[s, :, y], s_y.at[s], r_y.at[s], y_peer(j)[1])

    def block_v(s):
        return remote(vb.at[0], vb.at[s], s_b.at[s], r_b.at[s], ((c + s) % n_ctx, t))

    loop(1, half, lambda j: near_k(j).start())
    loop(1, steps, when_sends(lambda s: along_ctx(s).start()))
    loop(1, half, lambda j: near_v(j).start())
    for load in loads[2:4]:
        load.wait()
    sib_q = remote(qn.at[0], qn.at[1], sib_send.at[0], sib_recv.at[0], sib)
    sib_g = remote(gn.at[0], gn.at[1], sib_send.at[1], sib_recv.at[1], sib)
    sib_x = remote(xt.at[0, pl.ds(0, 16)], xt.at[1, pl.ds(0, 16)], sib_send.at[2], sib_recv.at[2], sib)
    sib_d = remote(dqt.at[1], dqs, sib_send.at[3], sib_recv.at[3], sib)
    sib_q.start()
    sib_g.start()

    for load in loads[4:]:
        load.wait()
    g_t = gn[0].T
    qt[0] = qn[0].T
    gt[0] = g_t
    delta = jnp.sum(g_t.astype(F32) * on[...].T.astype(F32), axis=0, keepdims=True)
    q_doc = jnp.concatenate([doc[pl.ds(c * lines + j, 1), :] for j in range(lines)], axis=1)
    place = lax.broadcasted_iota(jnp.int32, (8, rows), 0)
    extra = jnp.zeros((8, rows), F32)
    for i, row in enumerate((*split3(lse[...] * math.sqrt(hd)), *split3(delta))):
        extra = jnp.where(place == i, -row, extra)
    xt[0, 0:8, :] = jnp.where(place == q_doc, -FAR, 0.0).astype(BF16)
    xt[0, 8:16, :] = extra.astype(BF16)
    sib_x.start()

    loop(1, steps, when_has(lambda s: along_ctx(s).wait_recv()))
    loop(1, steps, when_has(lambda s: across_z(s).start()))

    for h in range(2):
        xt[h, 16:, :] = jnp.zeros((hd - 16, rows), BF16)
    turned = pltpu.roll(doc[...], 64, 1)
    doc_a[...] = jnp.where(core == 0, doc[...], turned)
    doc_b[...] = jnp.where(core == 0, turned, doc[...])
    lane = lax.broadcasted_iota(jnp.int32, (128, 128), 1)

    def features(s):
        for m in range(lines // 2):
            at = (c - s) * lines + 2 * m
            both = jnp.where(lane < 64, doc_a[pl.ds(at, 1), :], doc_b[pl.ds(at + 1, 1), :])
            other = jnp.where((lane < 11) & (both.T != lane), 1.0, 0.0)
            fk[s, m * 128:(m + 1) * 128, :] = other.astype(BF16)

    loop(0, steps, when_has(features))
    dqt[...] = jnp.zeros_like(dqt)

    await_bytes(rs_v, near_recv.at[1])
    loop(1, steps, when_sends(lambda s: block_v(s).start()))
    await_bytes(rs_v, near_recv.at[0])

    def spread_y(s):
        across_z(s).wait_recv()
        loop(1, ys, lambda j: along_y(s, j).start())

    v_lane = lax.broadcasted_iota(jnp.int32, (1, 128), 1)
    v_row = jnp.where((v_lane >= 11) & (v_lane < 14), 1.0, 0.0).astype(BF16)

    def tile(h, s, q0, tq, k0, tk, diagonal):
        qs, ks = pl.ds(q0, tq), pl.ds(k0, tk)
        x = xt[h, :, qs]
        k_own = kb[s].reshape(width, hd)[k0:k0 + tk]
        v_own = vb[s].reshape(width, hd)[k0:k0 + tk]
        k_all = jnp.concatenate([k_own, fk[s, ks]], axis=1)
        v_all = jnp.concatenate([v_own, jnp.broadcast_to(v_row, (tk, 128))], axis=1)
        prob = jnp.exp2(dot(k_all, jnp.concatenate([qt[h, :, qs], x], axis=0)) * (scale * math.log2(math.e)))
        if diagonal:
            r = k0 + lax.broadcasted_iota(jnp.int32, (tk, tq), 0)
            k_pos = (r // own * 2 + core) * own + r % own
            prob = jnp.where(k_pos <= q0 + lax.broadcasted_iota(jnp.int32, (tk, tq), 1), prob, 0.0)
        dprob = dot(v_all, jnp.concatenate([gt[h, :, qs], x], axis=0))
        low = prob.astype(BF16)
        dscore = (prob * dprob).astype(BF16)
        acc[0, ks] += dot(dscore, qn[h, qs])
        acc[1, ks] += dot(low, gn[h, qs])
        dqt[h, :, qs] += dot(k_own.T, dscore)

    def to_y(s, j):
        w, to = y_peer(j)
        return remote(part_k.at[s, :, w], rs_k.at[s, j - 1], s_p.at[s], r_p.at[s], to)

    def to_z(s):
        return remote(y_out.at[s], z_in.at[s], s_q.at[s], r_q.at[s], over_z)

    def to_owner(s):
        return remote(back.at[s], fin_k.at[s], s_f.at[s], r_f.at[s], ((c + n_ctx - s) % n_ctx, t))

    def v_to_owner(s):
        return remote(part_v.at[s], fin_v.at[s], s_g.at[s], r_g.at[s], ((c + n_ctx - s) % n_ctx, t))

    def hand_out(s):
        part_k[s] = acc[0].astype(BF16).reshape(2, ys, own, hd)
        loop(1, ys, lambda j: to_y(s, j).start())
        if isinstance(s, int) and s == 0:
            tot_v[...] = acc[1]
        else:
            part_v[s] = acc[1].astype(BF16)
            v_to_owner(s).start()

    def sum_y(s):
        await_bytes(rs_k.at[s], r_p.at[s])

        def total(at):
            full = part_k[s, at, y].astype(F32)
            for j in range(ys - 1):
                full += rs_k[s, j, at].astype(F32)
            return full
        y_own[s] = total(z)
        y_out[s] = total(1 - z).astype(BF16)
        to_z(s).start()

    def sum_z(s):
        to_z(s).wait_recv()
        full = y_own[s] + z_in[s].astype(F32)
        if isinstance(s, int) and s == 0:
            tot_k[...] = full
        else:
            back[s] = full.astype(BF16)
            to_owner(s).start()

    tq = min(256, rows)

    def edge(h, s):
        for q0 in range(0, rows, tq):
            if s == 0:
                tile(h, s, q0, tq, 0, (q0 + tq) // 2, True)
            else:
                tile(h, s, q0, tq, q0 // 2, width - q0 // 2, False)

    acc[...] = jnp.zeros_like(acc)
    edge(0, 0)
    loop(1, steps, when_has(spread_y))
    sib_q.wait_recv()
    sib_g.wait_recv()
    sib_x.wait_recv()
    qt[1] = qn[1].T
    gt[1] = gn[1].T
    edge(1, 0)
    hand_out(0)
    pl.when(c == 0)(lambda: sib_d.start())

    last = steps - 1 if (steps - 1) * rows == SPAN else steps

    def step(s):
        edged = isinstance(s, int) and s == last
        before = s - 1

        @pl.when(c >= s)
        def _():
            await_bytes(part_k.at[s, :, pl.ds(0, ys - 1)], r_y.at[s])
            block_v(s).wait_recv()
            acc[...] = jnp.zeros_like(acc)
            for h in (1, 0):
                if edged:
                    edge(h, s)
                else:
                    tile(h, s, 0, rows, 0, width, False)
                if h == 1:
                    @pl.when((c == s) | (s == steps - 1))
                    def _():
                        sib_d.start()
                    sum_y(before)
            hand_out(s)

        @pl.when(c == before)
        def _():
            sum_y(before)

        @pl.when(c >= before)
        def _():
            sum_z(before)

    if steps > 1:
        step(1)
    loop(2, last, step)
    if 1 < last < steps:
        step(last)

    @pl.when(c >= steps - 1)
    def _():
        sum_y(steps - 1)
        sum_z(steps - 1)

    sib_d.wait_recv()
    dq_out[...] = ((dqt[0] + dqs[...]) * scale).T.astype(BF16)

    def collect_v(s):
        v_to_owner(s).wait_recv()
        tot_v[...] += fin_v[s].astype(F32).reshape(width, hd)

    def collect_k(s):
        to_owner(s).wait_recv()
        tot_k[...] += fin_k[s].astype(F32)

    def last_v(j):
        pz, py, to = peer(j)
        return remote(out_v.at[pz, py], rs_v.at[j - 1], last_send, last_recv, to)

    loop(1, steps, when_sends(collect_v))
    out_v[...] = tot_v[...].astype(BF16).reshape(2, ys, own, hd)
    loop(1, half, lambda j: last_v(j).start())
    loop(1, steps, when_sends(collect_k))
    dk_out[...] = (tot_k[...] * scale).astype(BF16)
    await_bytes(rs_v, last_recv)
    full = out_v[z, y].astype(F32)
    for j in range(half - 1):
        full += rs_v[j].astype(F32)
    dv_out[...] = full.astype(BF16)

    for copy in (sib_q, sib_g, sib_x, sib_d):
        copy.wait_send()
    await_bytes(rs_v, near_send.at[0])
    await_bytes(rs_v, near_send.at[1])
    await_bytes(rs_v, last_send)

    def sent_down(s):
        along_ctx(s).wait_send()
        block_v(s).wait_send()

    def sent_up(s):
        across_z(s).wait_send()
        await_bytes(rs_k.at[s], s_y.at[s])
        to_owner(s).wait_send()
        v_to_owner(s).wait_send()

    def sent_sums(s):
        await_bytes(rs_k.at[s], s_p.at[s])
        to_z(s).wait_send()

    loop(1, steps, when_sends(sent_down))
    loop(1, steps, when_has(sent_up))
    loop(0, steps, when_has(sent_sums))


def body(n_ctx, n_tp, queries, keys, values, outputs, out_grad, log_norm, doc_ids):
    rows, hd = queries.shape
    own = keys.shape[0]
    half = n_tp // 2
    width = own * half
    steps = min(n_ctx, -(-SPAN // rows) + 1)
    doc_ids = doc_ids.reshape(-1, 128)
    dma = pltpu.SemaphoreType.DMA
    anywhere = pl.BlockSpec(memory_space=pl.ANY)
    inside = pl.BlockSpec(memory_space=pltpu.VMEM)
    return pl.pallas_call(
        functools.partial(kernel, n_ctx, n_tp, steps),
        out_shape=(
            jax.ShapeDtypeStruct((rows, hd), BF16),
            jax.ShapeDtypeStruct((own, hd), BF16),
            jax.ShapeDtypeStruct((own, hd), BF16),
        ),
        in_specs=[anywhere] * 7,
        out_specs=(inside, inside, inside),
        scratch_shapes=[
            pltpu.VMEM((2, rows, hd), BF16),
            pltpu.VMEM((2, rows, hd), BF16),
            pltpu.VMEM((rows, hd), BF16),
            pltpu.VMEM((2, hd, rows), BF16),
            pltpu.VMEM((2, hd, rows), BF16),
            pltpu.VMEM((2, hd, rows), BF16),
            pltpu.VMEM((steps, 2, half // 2, own, hd), BF16),
            pltpu.VMEM((steps, 2, half // 2, own, hd), BF16),
            pltpu.VMEM((steps, width, hd), BF16),
            pltpu.VMEM((2, width, hd), F32),
            pltpu.VMEM((2, hd, rows), F32),
            pltpu.VMEM((hd, rows), F32),
            pltpu.VMEM((steps, 2, half // 2, own, hd), BF16),
            pltpu.VMEM((steps, half // 2 - 1, 2, own, hd), BF16),
            pltpu.VMEM((steps, own, hd), BF16),
            pltpu.VMEM((steps, own, hd), F32),
            pltpu.VMEM((steps, own, hd), BF16),
            pltpu.VMEM((steps, own, hd), BF16),
            pltpu.VMEM((steps, own, hd), BF16),
            pltpu.VMEM((own, hd), F32),
            pltpu.VMEM((steps, width, hd), BF16),
            pltpu.VMEM((steps, width, hd), BF16),
            pltpu.VMEM((width, hd), F32),
            pltpu.VMEM((2, half // 2, own, hd), BF16),
            pltpu.VMEM((half - 1, own, hd), BF16),
            pltpu.VMEM((1, rows), F32),
            pltpu.VMEM(doc_ids.shape, jnp.int32),
            pltpu.VMEM(doc_ids.shape, jnp.int32),
            pltpu.VMEM(doc_ids.shape, jnp.int32),
            dma((7,)), dma((4,)), dma((4,)), dma((2,)), dma((2,)), dma, dma,
            *[dma((steps,)) for _ in range(16)],
        ],
        compiler_params=pltpu.CompilerParams(
            collective_id=0, has_side_effects=True, vmem_limit_bytes=63 * 1024 * 1024),
    )(queries, keys, values, outputs, out_grad, log_norm, doc_ids)


def solution(mesh):
    return jax.shard_map(
        functools.partial(body, mesh.shape["ctx"], mesh.shape["tp"]),
        mesh=mesh,
        in_specs=(
            P("ctx", "tp"),
            P(("ctx", "tp"), None),
            P(("ctx", "tp"), None),
            P("ctx", "tp"),
            P("ctx", "tp"),
            P("tp", "ctx"),
            P(),
        ),
        out_specs=(P("ctx", "tp"), P(("ctx", "tp"), None), P(("ctx", "tp"), None)),
        check_vma=False,
    )
```

time: 75 us -> 74.1 us (0.988)
  the two profiles are of different devices: /device:TPU:0 before, /device:TPU:2 now
where the time goes in v2:
time: 74.1 us; the launch traced here: 73.9 us
  Pallas kernels  70.2 us (95%)
  local copies, waits for them, and re-layouts  3.01 us (4%)
    pallas_call x1, Pallas kernels, body(): pl.pallas_call(functools.partial(kernel, n_ctx, n_tp, steps), out_shape=(...  70.2 us
    unnamed x7, local copies, waits for them, and re-layouts  3.01 us

profile of v2, /device:TPU:2, one launch (start us, length us, event | category | flops | bytes accessed | tf_op | source)
XLA Modules:
  0.0 73.9 jit_solution(10983751711868025206)
XLA Ops:
  0.6 70.2 %shard_map.94 = (bf16[1024,128]{1,0:T(8,128)(2,1)}, bf16[64,128]{1,0:T(8,128)(2,1)}, bf16[64,128]{1,0:T(8,128)(2,1)}) custom-call(bf16[1024,128]{1,0:T(8,128)(2,1)} %q_in.1, bf16[64,128]{1,0:T(8,128)(2,1)} %k_in.1, bf16[64,128]{1,0:T(8,128)(2,1)} %v_in.1, bf16[1024,128]{1,0:T(8,128)(2,1)} %o_in.1, bf16[1024,128]{1,0:T(8,128)(2,1)} %g_in.1, ...), custom_call_target="tpu_custom_call" | custom-call | tf_op jit(solution)/shard_map/pallas_call | solution.py:373
  70.9 0.0 copy-start.1
  70.9 1.7 %copy.13 = bf16[1024,128]{1,0:T(8,128)(2,1)} copy(bf16[1024,128]{1,0:T(8,128)(2,1)} %get-tuple-element.6) | data formatting | bytes 524288
  72.6 0.0 copy-done.1
  72.6 0.0 copy-start
  72.6 0.6 copy.14
  73.2 0.1 copy-done
  73.3 0.6 copy.15
Async XLA Ops:
  70.9 1.7 %copy-start.1 = (bf16[64,128]{1,0:T(8,128)(2,1)S(1)}, bf16[64,128]{1,0:T(8,128)(2,1)}, u32[]{:S(2)}) copy-start(bf16[64,128]{1,0:T(8,128)(2,1)} %get-tuple-element.7) | copy-start | bytes 49156
  72.6 0.7 copy-start

commit v3 on v2

--- a/solution.py
+++ b/solution.py
@@ -31,7 +31,7 @@
     dq_out, dk_out, dv_out,
     qn, gn, on, qt, gt, xt, kb, vb, fk, acc, dqt, dqs,
     part_k, rs_k, y_out, y_own, z_in, back, fin_k, tot_k,
-    part_v, fin_v, tot_v, out_v, rs_v,
+    part_v, fin_v, acc_own, out_k, out_v, own_k, rs_v,
     lse, doc, doc_a, doc_b,
     in_sem, sib_send, sib_recv, near_send, near_recv, last_send, last_recv,
     s_a, r_a, s_z, r_z, s_y, r_y, s_b, r_b, s_p, r_p, s_q, r_q, s_f, r_f, s_g, r_g,
@@ -68,6 +68,9 @@
             return 0
         lax.fori_loop(first, last, one, 0)
 
+    def down(fn):
+        loop(0, steps - 1, lambda i: fn(steps - 1 - i))
+
     def when_sends(fn):
         def run(s):
             @pl.when(c + s < n_ctx)
@@ -104,9 +107,6 @@
     greet(sib)
     loop(1, half, lambda j: greet(peer(j)[2]))
     loop(1, n_ctx, lambda j: greet(((c + j) % n_ctx, t)))
-    for load in loads[:2]:
-        load.wait()
-    pl.semaphore_wait(barrier, 1 + half - 1 + n_ctx - 1)
 
     def near_k(j):
         return remote(kb.at[0, z, y], kb.at[0, z, y], near_send.at[0], near_recv.at[0], peer(j)[2])
@@ -126,38 +126,35 @@
     def block_v(s):
         return remote(vb.at[0], vb.at[s], s_b.at[s], r_b.at[s], ((c + s) % n_ctx, t))
 
-    loop(1, half, lambda j: near_k(j).start())
-    loop(1, steps, when_sends(lambda s: along_ctx(s).start()))
-    loop(1, half, lambda j: near_v(j).start())
-    for load in loads[2:4]:
-        load.wait()
     sib_q = remote(qn.at[0], qn.at[1], sib_send.at[0], sib_recv.at[0], sib)
     sib_g = remote(gn.at[0], gn.at[1], sib_send.at[1], sib_recv.at[1], sib)
     sib_x = remote(xt.at[0, pl.ds(0, 16)], xt.at[1, pl.ds(0, 16)], sib_send.at[2], sib_recv.at[2], sib)
     sib_d = remote(dqt.at[1], dqs, sib_send.at[3], sib_recv.at[3], sib)
-    sib_q.start()
-    sib_g.start()
-
-    for load in loads[4:]:
+
+    for load in loads:
         load.wait()
-    g_t = gn[0].T
-    qt[0] = qn[0].T
-    gt[0] = g_t
-    delta = jnp.sum(g_t.astype(F32) * on[...].T.astype(F32), axis=0, keepdims=True)
     q_doc = jnp.concatenate([doc[pl.ds(c * lines + j, 1), :] for j in range(lines)], axis=1)
+    delta = jnp.sum(gn[0].T.astype(F32) * on[...].T.astype(F32), axis=0, keepdims=True)
     place = lax.broadcasted_iota(jnp.int32, (8, rows), 0)
     extra = jnp.zeros((8, rows), F32)
     for i, row in enumerate((*split3(lse[...] * math.sqrt(hd)), *split3(delta))):
         extra = jnp.where(place == i, -row, extra)
     xt[0, 0:8, :] = jnp.where(place == q_doc, -FAR, 0.0).astype(BF16)
     xt[0, 8:16, :] = extra.astype(BF16)
+
+    pl.semaphore_wait(barrier, 1 + half - 1 + n_ctx - 1)
+    down(when_sends(lambda s: along_ctx(s).start()))
+    loop(1, half, lambda j: near_v(j).start())
+    loop(1, half, lambda j: near_k(j).start())
     sib_x.start()
-
-    loop(1, steps, when_has(lambda s: along_ctx(s).wait_recv()))
-    loop(1, steps, when_has(lambda s: across_z(s).start()))
-
+    sib_q.start()
+    sib_g.start()
+
+    qt[0] = qn[0].T
+    gt[0] = gn[0].T
     for h in range(2):
         xt[h, 16:, :] = jnp.zeros((hd - 16, rows), BF16)
+    dqt[...] = jnp.zeros_like(dqt)
     turned = pltpu.roll(doc[...], 64, 1)
     doc_a[...] = jnp.where(core == 0, doc[...], turned)
     doc_b[...] = jnp.where(core == 0, turned, doc[...])
@@ -170,21 +167,29 @@
             other = jnp.where((lane < 11) & (both.T != lane), 1.0, 0.0)
             fk[s, m * 128:(m + 1) * 128, :] = other.astype(BF16)
 
-    loop(0, steps, when_has(features))
-    dqt[...] = jnp.zeros_like(dqt)
+    features(0)
+    down(when_has(lambda s: along_ctx(s).wait_recv()))
+    down(when_has(lambda s: across_z(s).start()))
+    sib_x.wait_recv()
+    sib_q.wait_recv()
+    sib_g.wait_recv()
+    qt[1] = qn[1].T
+    gt[1] = gn[1].T
 
     await_bytes(rs_v, near_recv.at[1])
-    loop(1, steps, when_sends(lambda s: block_v(s).start()))
+    down(when_sends(lambda s: block_v(s).start()))
     await_bytes(rs_v, near_recv.at[0])
 
     def spread_y(s):
         across_z(s).wait_recv()
         loop(1, ys, lambda j: along_y(s, j).start())
 
+    down(when_has(spread_y))
+
     v_lane = lax.broadcasted_iota(jnp.int32, (1, 128), 1)
     v_row = jnp.where((v_lane >= 11) & (v_lane < 14), 1.0, 0.0).astype(BF16)
 
-    def tile(h, s, q0, tq, k0, tk, diagonal):
+    def tile(h, s, q0, tq, k0, tk, diagonal, sums):
         qs, ks = pl.ds(q0, tq), pl.ds(k0, tk)
         x = xt[h, :, qs]
         k_own = kb[s].reshape(width, hd)[k0:k0 + tk]
@@ -199,8 +204,8 @@
         dprob = dot(v_all, jnp.concatenate([gt[h, :, qs], x], axis=0))
         low = prob.astype(BF16)
         dscore = (prob * dprob).astype(BF16)
-        acc[0, ks] += dot(dscore, qn[h, qs])
-        acc[1, ks] += dot(low, gn[h, qs])
+        sums[0, ks] += dot(dscore, qn[h, qs])
+        sums[1, ks] += dot(low, gn[h, qs])
         dqt[h, :, qs] += dot(k_own.T, dscore)
 
     def to_y(s, j):
@@ -219,11 +224,8 @@
     def hand_out(s):
         part_k[s] = acc[0].astype(BF16).reshape(2, ys, own, hd)
         loop(1, ys, lambda j: to_y(s, j).start())
-        if isinstance(s, int) and s == 0:
-            tot_v[...] = acc[1]
-        else:
-            part_v[s] = acc[1].astype(BF16)
-            v_to_owner(s).start()
+        part_v[s] = acc[1].astype(BF16)
+        v_to_owner(s).start()
 
     def sum_y(s):
         await_bytes(rs_k.at[s], r_p.at[s])
@@ -239,97 +241,105 @@
 
     def sum_z(s):
         to_z(s).wait_recv()
-        full = y_own[s] + z_in[s].astype(F32)
-        if isinstance(s, int) and s == 0:
-            tot_k[...] = full
-        else:
-            back[s] = full.astype(BF16)
-            to_owner(s).start()
+        back[s] = (y_own[s] + z_in[s].astype(F32)).astype(BF16)
+        to_owner(s).start()
 
     tq = min(256, rows)
 
-    def edge(h, s):
+    def edge(h, s, sums):
         for q0 in range(0, rows, tq):
             if s == 0:
-                tile(h, s, q0, tq, 0, (q0 + tq) // 2, True)
+                tile(h, s, q0, tq, 0, (q0 + tq) // 2, True, sums)
             else:
-                tile(h, s, q0, tq, q0 // 2, width - q0 // 2, False)
-
-    acc[...] = jnp.zeros_like(acc)
-    edge(0, 0)
-    loop(1, steps, when_has(spread_y))
-    sib_q.wait_recv()
-    sib_g.wait_recv()
-    sib_x.wait_recv()
-    qt[1] = qn[1].T
-    gt[1] = gn[1].T
-    edge(1, 0)
-    hand_out(0)
+                tile(h, s, q0, tq, q0 // 2, width - q0 // 2, False, sums)
+
+    acc_own[...] = jnp.zeros_like(acc_own)
+    edge(1, 0, acc_own)
     pl.when(c == 0)(lambda: sib_d.start())
-
-    last = steps - 1 if (steps - 1) * rows == SPAN else steps
-
-    def step(s):
-        edged = isinstance(s, int) and s == last
-        before = s - 1
-
+    down(when_has(features))
+
+    def once(s, fn):
+        if isinstance(s, int) and s >= steps:
+            return
+
+        @pl.when((c >= s) & (s < steps))
+        def _():
+            fn(s)
+
+    def step(s, edged):
         @pl.when(c >= s)
         def _():
             await_bytes(part_k.at[s, :, pl.ds(0, ys - 1)], r_y.at[s])
             block_v(s).wait_recv()
             acc[...] = jnp.zeros_like(acc)
-            for h in (1, 0):
-                if edged:
-                    edge(h, s)
-                else:
-                    tile(h, s, 0, rows, 0, width, False)
-                if h == 1:
-                    @pl.when((c == s) | (s == steps - 1))
-                    def _():
-                        sib_d.start()
-                    sum_y(before)
+            if edged:
+                edge(1, s, acc)
+            else:
+                tile(1, s, 0, rows, 0, width, False, acc)
+            if not isinstance(s, int) or s == 1:
+                @pl.when(s == 1)
+                def _():
+                    sib_d.start()
+
+        once(s + 2, sum_y)
+        once(s + 3, sum_z)
+
+        @pl.when(c >= s)
+        def _():
+            if edged:
+                edge(0, s, acc)
+            else:
+                tile(0, s, 0, rows, 0, width, False, acc)
             hand_out(s)
 
-        @pl.when(c == before)
-        def _():
-            sum_y(before)
-
-        @pl.when(c >= before)
-        def _():
-            sum_z(before)
-
-    if steps > 1:
-        step(1)
-    loop(2, last, step)
-    if 1 < last < steps:
-        step(last)
-
-    @pl.when(c >= steps - 1)
-    def _():
-        sum_y(steps - 1)
-        sum_z(steps - 1)
+    first = steps - 1
+    if first * rows == SPAN:
+        step(first, True)
+        first -= 1
+    loop(0, first, lambda i: step(first - i, False))
+
+    if steps > 2:
+        once(2, sum_y)
+    edge(0, 0, acc_own)
+    out_k[...] = acc_own[0].astype(BF16).reshape(2, ys, own, hd)
+
+    def last_k(j):
+        pz, py, to = peer(j)
+        return remote(out_k.at[pz, py], own_k.at[j - 1], last_send.at[0], last_recv.at[0], to)
+
+    def last_v(j):
+        pz, py, to = peer(j)
+        return remote(out_v.at[pz, py], rs_v.at[j - 1], last_send.at[1], last_recv.at[1], to)
+
+    def collect_v(s):
+        v_to_owner(s).wait_recv()
+        acc_own[1] += fin_v[s].astype(F32)
+
+    loop(1, half, lambda j: last_k(j).start())
+    once(3, sum_z)
+    once(1, sum_y)
+    once(2, sum_z)
+    once(1, sum_z)
+    down(when_sends(collect_v))
+    out_v[...] = acc_own[1].astype(BF16).reshape(2, ys, own, hd)
+    loop(1, half, lambda j: last_v(j).start())
 
     sib_d.wait_recv()
     dq_out[...] = ((dqt[0] + dqs[...]) * scale).T.astype(BF16)
 
-    def collect_v(s):
-        v_to_owner(s).wait_recv()
-        tot_v[...] += fin_v[s].astype(F32).reshape(width, hd)
+    await_bytes(rs_v, last_recv.at[0])
+    full = out_k[z, y].astype(F32)
+    for j in range(half - 1):
+        full += own_k[j].astype(F32)
+    tot_k[...] = full
 
     def collect_k(s):
         to_owner(s).wait_recv()
         tot_k[...] += fin_k[s].astype(F32)
 
-    def last_v(j):
-        pz, py, to = peer(j)
-        return remote(out_v.at[pz, py], rs_v.at[j - 1], last_send, last_recv, to)
-
-    loop(1, steps, when_sends(collect_v))
-    out_v[...] = tot_v[...].astype(BF16).reshape(2, ys, own, hd)
-    loop(1, half, lambda j: last_v(j).start())
-    loop(1, steps, when_sends(collect_k))
+    down(when_sends(collect_k))
     dk_out[...] = (tot_k[...] * scale).astype(BF16)
-    await_bytes(rs_v, last_recv)
+    await_bytes(rs_v, last_recv.at[1])
     full = out_v[z, y].astype(F32)
     for j in range(half - 1):
         full += rs_v[j].astype(F32)
@@ -337,9 +347,9 @@
 
     for copy in (sib_q, sib_g, sib_x, sib_d):
         copy.wait_send()
-    await_bytes(rs_v, near_send.at[0])
-    await_bytes(rs_v, near_send.at[1])
-    await_bytes(rs_v, last_send)
+    for i in range(2):
+        await_bytes(rs_v, near_send.at[i])
+        await_bytes(rs_v, last_send.at[i])
 
     def sent_down(s):
         along_ctx(s).wait_send()
@@ -350,14 +360,11 @@
         await_bytes(rs_k.at[s], s_y.at[s])
         to_owner(s).wait_send()
         v_to_owner(s).wait_send()
-
-    def sent_sums(s):
         await_bytes(rs_k.at[s], s_p.at[s])
         to_z(s).wait_send()
 
-    loop(1, steps, when_sends(sent_down))
-    loop(1, steps, when_has(sent_up))
-    loop(0, steps, when_has(sent_sums))
+    down(when_sends(sent_down))
+    down(when_has(sent_up))
 
 
 def body(n_ctx, n_tp, queries, keys, values, outputs, out_grad, log_norm, doc_ids):
@@ -402,14 +409,16 @@
             pltpu.VMEM((own, hd), F32),
             pltpu.VMEM((steps, width, hd), BF16),
             pltpu.VMEM((steps, width, hd), BF16),
-            pltpu.VMEM((width, hd), F32),
+            pltpu.VMEM((2, width, hd), F32),
             pltpu.VMEM((2, half // 2, own, hd), BF16),
+            pltpu.VMEM((2, half // 2, own, hd), BF16),
+            pltpu.VMEM((half - 1, own, hd), BF16),
             pltpu.VMEM((half - 1, own, hd), BF16),
             pltpu.VMEM((1, rows), F32),
             pltpu.VMEM(doc_ids.shape, jnp.int32),
             pltpu.VMEM(doc_ids.shape, jnp.int32),
             pltpu.VMEM(doc_ids.shape, jnp.int32),
-            dma((7,)), dma((4,)), dma((4,)), dma((2,)), dma((2,)), dma, dma,
+            dma((7,)), dma((4,)), dma((4,)), dma((2,)), dma((2,)), dma((2,)), dma((2,)),
             *[dma((steps,)) for _ in range(16)],
         ],
         compiler_params=pltpu.CompilerParams(

time: 74.1 us -> 58.1 us (0.78)
  the two profiles are of different devices: /device:TPU:2 before, /device:TPU:38 now
where the time goes in v3:
time: 58.1 us; the launch traced here: 57.8 us
  Pallas kernels  54.2 us (93%)
  local copies, waits for them, and re-layouts  3.01 us (5%)
  between operations  0.65 us (1%)
    pallas_call x1, Pallas kernels, body(): pl.pallas_call(functools.partial(kernel, n_ctx, n_tp, steps), out_shape=(...  54.2 us
    unnamed x7, local copies, waits for them, and re-layouts  3.01 us

profile of v3, /device:TPU:38, one launch (start us, length us, event | category | flops | bytes accessed | tf_op | source)
XLA Modules:
  0.0 57.8 jit_solution(11304589461320043927)
XLA Ops:
  0.6 54.2 %shard_map.94 = (bf16[1024,128]{1,0:T(8,128)(2,1)}, bf16[64,128]{1,0:T(8,128)(2,1)}, bf16[64,128]{1,0:T(8,128)(2,1)}) custom-call(bf16[1024,128]{1,0:T(8,128)(2,1)} %q_in.1, bf16[64,128]{1,0:T(8,128)(2,1)} %k_in.1, bf16[64,128]{1,0:T(8,128)(2,1)} %v_in.1, bf16[1024,128]{1,0:T(8,128)(2,1)} %o_in.1, bf16[1024,128]{1,0:T(8,128)(2,1)} %g_in.1, ...), custom_call_target="tpu_custom_call" | custom-call | tf_op jit(solution)/shard_map/pallas_call | solution.py:380
  54.8 0.0 copy-start.1
  54.8 1.7 %copy.13 = bf16[1024,128]{1,0:T(8,128)(2,1)} copy(bf16[1024,128]{1,0:T(8,128)(2,1)} %get-tuple-element.6) | data formatting | bytes 524288
  56.5 0.0 copy-done.1
  56.5 0.0 copy-start
  56.5 0.6 %copy.14 = bf16[64,128]{1,0:T(8,128)(2,1)} copy(bf16[64,128]{1,0:T(8,128)(2,1)S(1)} %copy-done.1) | data formatting | bytes 32768
  57.1 0.1 copy-done
  57.2 0.6 %copy.15 = bf16[64,128]{1,0:T(8,128)(2,1)} copy(bf16[64,128]{1,0:T(8,128)(2,1)S(1)} %copy-done) | data formatting | bytes 32768
Async XLA Ops:
  54.8 1.7 %copy-start.1 = (bf16[64,128]{1,0:T(8,128)(2,1)S(1)}, bf16[64,128]{1,0:T(8,128)(2,1)}, u32[]{:S(2)}) copy-start(bf16[64,128]{1,0:T(8,128)(2,1)} %get-tuple-element.7) | copy-start | bytes 49156
  56.5 0.7 %copy-start = (bf16[64,128]{1,0:T(8,128)(2,1)S(1)}, bf16[64,128]{1,0:T(8,128)(2,1)}, u32[]{:S(2)}) copy-start(bf16[64,128]{1,0:T(8,128)(2,1)} %get-tuple-element.8) | copy-start | bytes 49156

commit v4 on v3

--- a/solution.py
+++ b/solution.py
@@ -31,9 +31,9 @@
     dq_out, dk_out, dv_out,
     qn, gn, on, qt, gt, xt, kb, vb, fk, acc, dqt, dqs,
     part_k, rs_k, y_out, y_own, z_in, back, fin_k, tot_k,
-    part_v, fin_v, acc_own, out_k, out_v, own_k, rs_v,
+    part_v, fin_v, acc_own, out_k, out_v, own_k, rs_v, one_k, one_v, sum_v, tot,
     lse, doc, doc_a, doc_b,
-    in_sem, sib_send, sib_recv, near_send, near_recv, last_send, last_recv,
+    in_sem, sib_send, sib_recv, near_send, near_recv, last_send, last_recv, one_send, one_recv,
     s_a, r_a, s_z, r_z, s_y, r_y, s_b, r_b, s_p, r_p, s_q, r_q, s_f, r_f, s_g, r_g,
 ):
     rows, hd = qn.shape[1], qn.shape[2]
@@ -131,7 +131,17 @@
     sib_x = remote(xt.at[0, pl.ds(0, 16)], xt.at[1, pl.ds(0, 16)], sib_send.at[2], sib_recv.at[2], sib)
     sib_d = remote(dqt.at[1], dqs, sib_send.at[3], sib_recv.at[3], sib)
 
-    for load in loads:
+    for load in loads[:2]:
+        load.wait()
+    pl.semaphore_wait(barrier, 1 + half - 1 + n_ctx - 1)
+    down(when_sends(lambda s: along_ctx(s).start()))
+    loop(1, half, lambda j: near_v(j).start())
+    for load in loads[2:4]:
+        load.wait()
+    sib_q.start()
+    sib_g.start()
+    loop(1, half, lambda j: near_k(j).start())
+    for load in loads[4:]:
         load.wait()
     q_doc = jnp.concatenate([doc[pl.ds(c * lines + j, 1), :] for j in range(lines)], axis=1)
     delta = jnp.sum(gn[0].T.astype(F32) * on[...].T.astype(F32), axis=0, keepdims=True)
@@ -142,13 +152,7 @@
     xt[0, 0:8, :] = jnp.where(place == q_doc, -FAR, 0.0).astype(BF16)
     xt[0, 8:16, :] = extra.astype(BF16)
 
-    pl.semaphore_wait(barrier, 1 + half - 1 + n_ctx - 1)
-    down(when_sends(lambda s: along_ctx(s).start()))
-    loop(1, half, lambda j: near_v(j).start())
-    loop(1, half, lambda j: near_k(j).start())
     sib_x.start()
-    sib_q.start()
-    sib_g.start()
 
     qt[0] = qn[0].T
     gt[0] = gn[0].T
@@ -177,14 +181,23 @@
     gt[1] = gn[1].T
 
     await_bytes(rs_v, near_recv.at[1])
-    down(when_sends(lambda s: block_v(s).start()))
-    await_bytes(rs_v, near_recv.at[0])
 
     def spread_y(s):
         across_z(s).wait_recv()
         loop(1, ys, lambda j: along_y(s, j).start())
 
-    down(when_has(spread_y))
+    ahead = 2
+
+    def wave_v(s):
+        @pl.when((c + s + ahead < n_ctx) & (s + ahead < steps))
+        def _():
+            block_v(s + ahead).wait_send()
+        block_v(s).start()
+
+    lead = max(steps - 1 - ahead, 0)
+    loop(0, steps - 1 - lead, lambda i: when_sends(wave_v)(steps - 1 - i))
+    loop(0, steps - 1 - lead, lambda i: when_has(spread_y)(steps - 1 - i))
+    await_bytes(rs_v, near_recv.at[0])
 
     v_lane = lax.broadcasted_iota(jnp.int32, (1, 128), 1)
     v_row = jnp.where((v_lane >= 11) & (v_lane < 14), 1.0, 0.0).astype(BF16)
@@ -221,11 +234,25 @@
     def v_to_owner(s):
         return remote(part_v.at[s], fin_v.at[s], s_g.at[s], r_g.at[s], ((c + n_ctx - s) % n_ctx, t))
 
+    def straight(i, src, dst, j):
+        pz, py, to = peer(j)
+        to = ((c + n_ctx - 1) % n_ctx, to[1])
+        return remote(src.at[pz, py], dst.at[j], one_send.at[i], one_recv.at[i], to)
+
     def hand_out(s):
         part_k[s] = acc[0].astype(BF16).reshape(2, ys, own, hd)
-        loop(1, ys, lambda j: to_y(s, j).start())
-        part_v[s] = acc[1].astype(BF16)
-        v_to_owner(s).start()
+
+        @pl.when(s == 1)
+        def _():
+            loop(0, half, lambda j: straight(0, part_k.at[1], one_k, j).start())
+            out_v[...] = acc[1].astype(BF16).reshape(2, ys, own, hd)
+            loop(0, half, lambda j: straight(1, out_v, one_v, j).start())
+
+        @pl.when(s > 1)
+        def _():
+            loop(1, ys, lambda j: to_y(s, j).start())
+            part_v[s] = acc[1].astype(BF16)
+            v_to_owner(s).start()
 
     def sum_y(s):
         await_bytes(rs_k.at[s], r_p.at[s])
@@ -267,6 +294,11 @@
             fn(s)
 
     def step(s, edged):
+        @pl.when(s > ahead)
+        def _():
+            when_sends(wave_v)(s - ahead)
+            when_has(spread_y)(s - ahead)
+
         @pl.when(c >= s)
         def _():
             await_bytes(part_k.at[s, :, pl.ds(0, ys - 1)], r_y.at[s])
@@ -309,62 +341,83 @@
 
     def last_v(j):
         pz, py, to = peer(j)
-        return remote(out_v.at[pz, py], rs_v.at[j - 1], last_send.at[1], last_recv.at[1], to)
+        return remote(sum_v.at[pz, py], rs_v.at[j - 1], last_send.at[1], last_recv.at[1], to)
 
     def collect_v(s):
         v_to_owner(s).wait_recv()
         acc_own[1] += fin_v[s].astype(F32)
 
+    def far(fn):
+        loop(0, steps - 2, lambda i: fn(steps - 1 - i))
+
     loop(1, half, lambda j: last_k(j).start())
     once(3, sum_z)
-    once(1, sum_y)
     once(2, sum_z)
-    once(1, sum_z)
-    down(when_sends(collect_v))
-    out_v[...] = acc_own[1].astype(BF16).reshape(2, ys, own, hd)
+    far(when_sends(collect_v))
+    sum_v[...] = acc_own[1].astype(BF16).reshape(2, ys, own, hd)
     loop(1, half, lambda j: last_v(j).start())
 
     sib_d.wait_recv()
     dq_out[...] = ((dqt[0] + dqs[...]) * scale).T.astype(BF16)
 
-    await_bytes(rs_v, last_recv.at[0])
-    full = out_k[z, y].astype(F32)
-    for j in range(half - 1):
-        full += own_k[j].astype(F32)
-    tot_k[...] = full
-
-    def collect_k(s):
-        to_owner(s).wait_recv()
-        tot_k[...] += fin_k[s].astype(F32)
-
-    down(when_sends(collect_k))
-    dk_out[...] = (tot_k[...] * scale).astype(BF16)
-    await_bytes(rs_v, last_recv.at[1])
-    full = out_v[z, y].astype(F32)
-    for j in range(half - 1):
-        full += rs_v[j].astype(F32)
-    dv_out[...] = full.astype(BF16)
-
     for copy in (sib_q, sib_g, sib_x, sib_d):
         copy.wait_send()
-    for i in range(2):
-        await_bytes(rs_v, near_send.at[i])
-        await_bytes(rs_v, last_send.at[i])
 
     def sent_down(s):
         along_ctx(s).wait_send()
-        block_v(s).wait_send()
-
-    def sent_up(s):
+
+        @pl.when(s <= ahead)
+        def _():
+            block_v(s).wait_send()
+
+    def sent_near(s):
         across_z(s).wait_send()
         await_bytes(rs_k.at[s], s_y.at[s])
+
+    def sent_up(s):
         to_owner(s).wait_send()
         v_to_owner(s).wait_send()
         await_bytes(rs_k.at[s], s_p.at[s])
         to_z(s).wait_send()
 
     down(when_sends(sent_down))
-    down(when_has(sent_up))
+    down(when_has(sent_near))
+    far(when_has(sent_up))
+
+    def collect_k(s):
+        to_owner(s).wait_recv()
+        tot_k[...] += fin_k[s].astype(F32)
+
+    tot_k[...] = out_k[z, y].astype(F32)
+    far(when_sends(collect_k))
+    for i in range(2):
+        await_bytes(rs_v, near_send.at[i])
+
+    @pl.when(c >= 1)
+    def _():
+        for i in range(2):
+            await_bytes(one_k, one_send.at[i])
+
+    def gathered(i, total, mine, ahead_of):
+        await_bytes(rs_v, last_recv.at[i])
+        for j in range(half - 1):
+            total += mine[j].astype(F32)
+        tot[i] = total
+
+        @pl.when(c + 1 < n_ctx)
+        def _():
+            await_bytes(one_k, one_recv.at[i])
+            more = ahead_of[0].astype(F32)
+            for j in range(1, half):
+                more += ahead_of[j].astype(F32)
+            tot[i] += more
+
+    gathered(0, tot_k[...], own_k, one_k)
+    dk_out[...] = (tot[0] * scale).astype(BF16)
+    gathered(1, sum_v[z, y].astype(F32), rs_v, one_v)
+    dv_out[...] = tot[1].astype(BF16)
+    for i in range(2):
+        await_bytes(rs_v, last_send.at[i])
 
 
 def body(n_ctx, n_tp, queries, keys, values, outputs, out_grad, log_norm, doc_ids):
@@ -414,11 +467,15 @@
             pltpu.VMEM((2, half // 2, own, hd), BF16),
             pltpu.VMEM((half - 1, own, hd), BF16),
             pltpu.VMEM((half - 1, own, hd), BF16),
+            pltpu.VMEM((half, own, hd), BF16),
+            pltpu.VMEM((half, own, hd), BF16),
+            pltpu.VMEM((2, half // 2, own, hd), BF16),
+            pltpu.VMEM((2, own, hd), F32),
             pltpu.VMEM((1, rows), F32),
             pltpu.VMEM(doc_ids.shape, jnp.int32),
             pltpu.VMEM(doc_ids.shape, jnp.int32),
             pltpu.VMEM(doc_ids.shape, jnp.int32),
-            dma((7,)), dma((4,)), dma((4,)), dma((2,)), dma((2,)), dma((2,)), dma((2,)),
+            dma((7,)), dma((4,)), dma((4,)), *[dma((2,)) for _ in range(6)],
             *[dma((steps,)) for _ in range(16)],
         ],
         compiler_params=pltpu.CompilerParams(

time: 58.1 us -> 51.1 us (0.88)
  the two profiles are of different devices: /device:TPU:38 before, /device:TPU:6 now
where the time goes in v4:
time: 51.1 us; the launch traced here: 50.9 us
  Pallas kernels  47.2 us (92%)
  local copies, waits for them, and re-layouts  3.01 us (6%)
  between operations  0.65 us (1%)
    pallas_call x1, Pallas kernels, body(): pl.pallas_call(functools.partial(kernel, n_ctx, n_tp, steps), out_shape=(...  47.2 us
    unnamed x7, local copies, waits for them, and re-layouts  3.01 us

profile of v4, /device:TPU:6, one launch (start us, length us, event | category | flops | bytes accessed | tf_op | source)
XLA Modules:
  0.0 50.9 jit_solution(16204609192481957640)
XLA Ops:
  0.6 47.2 %shard_map.94 = (bf16[1024,128]{1,0:T(8,128)(2,1)}, bf16[64,128]{1,0:T(8,128)(2,1)}, bf16[64,128]{1,0:T(8,128)(2,1)}) custom-call(bf16[1024,128]{1,0:T(8,128)(2,1)} %q_in.1, bf16[64,128]{1,0:T(8,128)(2,1)} %k_in.1, bf16[64,128]{1,0:T(8,128)(2,1)} %v_in.1, bf16[1024,128]{1,0:T(8,128)(2,1)} %o_in.1, bf16[1024,128]{1,0:T(8,128)(2,1)} %g_in.1, ...), custom_call_target="tpu_custom_call" | custom-call | tf_op jit(solution)/shard_map/pallas_call | solution.py:433
  47.8 0.0 copy-start.1
  47.8 1.7 %copy.13 = bf16[1024,128]{1,0:T(8,128)(2,1)} copy(bf16[1024,128]{1,0:T(8,128)(2,1)} %get-tuple-element.6) | data formatting | bytes 524288
  49.5 0.0 copy-done.1
  49.5 0.0 copy-start
  49.5 0.6 %copy.14 = bf16[64,128]{1,0:T(8,128)(2,1)} copy(bf16[64,128]{1,0:T(8,128)(2,1)S(1)} %copy-done.1) | data formatting | bytes 32768
  50.1 0.1 copy-done
  50.3 0.6 %copy.15 = bf16[64,128]{1,0:T(8,128)(2,1)} copy(bf16[64,128]{1,0:T(8,128)(2,1)S(1)} %copy-done) | data formatting | bytes 32768
Async XLA Ops:
  47.8 1.7 %copy-start.1 = (bf16[64,128]{1,0:T(8,128)(2,1)S(1)}, bf16[64,128]{1,0:T(8,128)(2,1)}, u32[]{:S(2)}) copy-start(bf16[64,128]{1,0:T(8,128)(2,1)} %get-tuple-element.7) | copy-start | bytes 49156
  49.5 0.7 %copy-start = (bf16[64,128]{1,0:T(8,128)(2,1)S(1)}, bf16[64,128]{1,0:T(8,128)(2,1)}, u32[]{:S(2)}) copy-start(bf16[64,128]{1,0:T(8,128)(2,1)} %get-tuple-element.8) | copy-start | bytes 49156

commit v5 on v4

--- a/solution.py
+++ b/solution.py
@@ -196,7 +196,7 @@
 
     lead = max(steps - 1 - ahead, 0)
     loop(0, steps - 1 - lead, lambda i: when_sends(wave_v)(steps - 1 - i))
-    loop(0, steps - 1 - lead, lambda i: when_has(spread_y)(steps - 1 - i))
+    down(when_has(spread_y))
     await_bytes(rs_v, near_recv.at[0])
 
     v_lane = lax.broadcasted_iota(jnp.int32, (1, 128), 1)
@@ -283,6 +283,18 @@
     acc_own[...] = jnp.zeros_like(acc_own)
     edge(1, 0, acc_own)
     pl.when(c == 0)(lambda: sib_d.start())
+    edge(0, 0, acc_own)
+    out_k[...] = acc_own[0].astype(BF16).reshape(2, ys, own, hd)
+
+    def last_k(j):
+        pz, py, to = peer(j)
+        return remote(out_k.at[pz, py], own_k.at[j - 1], last_send.at[0], last_recv.at[0], to)
+
+    def last_v(j):
+        pz, py, to = peer(j)
+        return remote(sum_v.at[pz, py], rs_v.at[j - 1], last_send.at[1], last_recv.at[1], to)
+
+    loop(1, half, lambda j: last_k(j).start())
     down(when_has(features))
 
     def once(s, fn):
@@ -297,7 +309,6 @@
         @pl.when(s > ahead)
         def _():
             when_sends(wave_v)(s - ahead)
-            when_has(spread_y)(s - ahead)
 
         @pl.when(c >= s)
         def _():
@@ -332,17 +343,6 @@
 
     if steps > 2:
         once(2, sum_y)
-    edge(0, 0, acc_own)
-    out_k[...] = acc_own[0].astype(BF16).reshape(2, ys, own, hd)
-
-    def last_k(j):
-        pz, py, to = peer(j)
-        return remote(out_k.at[pz, py], own_k.at[j - 1], last_send.at[0], last_recv.at[0], to)
-
-    def last_v(j):
-        pz, py, to = peer(j)
-        return remote(sum_v.at[pz, py], rs_v.at[j - 1], last_send.at[1], last_recv.at[1], to)
-
     def collect_v(s):
         v_to_owner(s).wait_recv()
         acc_own[1] += fin_v[s].astype(F32)
@@ -350,12 +350,11 @@
     def far(fn):
         loop(0, steps - 2, lambda i: fn(steps - 1 - i))
 
-    loop(1, half, lambda j: last_k(j).start())
     once(3, sum_z)
-    once(2, sum_z)
     far(when_sends(collect_v))
     sum_v[...] = acc_own[1].astype(BF16).reshape(2, ys, own, hd)
     loop(1, half, lambda j: last_v(j).start())
+    once(2, sum_z)
 
     sib_d.wait_recv()
     dq_out[...] = ((dqt[0] + dqs[...]) * scale).T.astype(BF16)
@@ -418,6 +417,12 @@
     dv_out[...] = tot[1].astype(BF16)
     for i in range(2):
         await_bytes(rs_v, last_send.at[i])
+
+
+def hand_over(*refs):
+    half = len(refs) // 2
+    for src, dst in zip(refs[:half], refs[half:]):
+        dst[...] = src[...]
 
 
 def body(n_ctx, n_tp, queries, keys, values, outputs, out_grad, log_norm, doc_ids):
@@ -430,7 +435,7 @@
     dma = pltpu.SemaphoreType.DMA
     anywhere = pl.BlockSpec(memory_space=pl.ANY)
     inside = pl.BlockSpec(memory_space=pltpu.VMEM)
-    return pl.pallas_call(
+    grads = pl.pallas_call(
         functools.partial(kernel, n_ctx, n_tp, steps),
         out_shape=(
             jax.ShapeDtypeStruct((rows, hd), BF16),
@@ -481,6 +486,12 @@
         compiler_params=pltpu.CompilerParams(
             collective_id=0, has_side_effects=True, vmem_limit_bytes=63 * 1024 * 1024),
     )(queries, keys, values, outputs, out_grad, log_norm, doc_ids)
+    return pl.pallas_call(
+        hand_over,
+        out_shape=tuple(jax.ShapeDtypeStruct(x.shape, x.dtype) for x in grads),
+        in_specs=[inside] * 3,
+        out_specs=(inside,) * 3,
+    )(*grads)
 
 
 def solution(mesh):

time: 51.1 us -> 48 us (0.939)
  the two profiles are of different devices: /device:TPU:6 before, /device:TPU:4 now
where the time goes in v5:
time: 48 us; the launch traced here: 47.8 us
  Pallas kernels  47.2 us (98%)
  between operations  0.64 us (1%)
    pallas_call x1, Pallas kernels, body(): pl.pallas_call(functools.partial(kernel, n_ctx, n_tp, steps), out_shape=(...  45.5 us
    pallas_call x1, Pallas kernels, body(): pl.pallas_call(hand_over, out_shape=tuple((jax.ShapeDtypeStruct(x.shape,...  1.69 us

profile of v5, /device:TPU:4, one launch (start us, length us, event | category | flops | bytes accessed | tf_op | source)
XLA Modules:
  0.0 47.8 jit_solution(1527724896352661393)
XLA Ops:
  0.6 45.5 %shard_map.94 = (bf16[1024,128]{1,0:T(8,128)(2,1)}, bf16[64,128]{1,0:T(8,128)(2,1)}, bf16[64,128]{1,0:T(8,128)(2,1)}) custom-call(bf16[1024,128]{1,0:T(8,128)(2,1)} %q_in.1, bf16[64,128]{1,0:T(8,128)(2,1)} %k_in.1, bf16[64,128]{1,0:T(8,128)(2,1)} %v_in.1, bf16[1024,128]{1,0:T(8,128)(2,1)} %o_in.1, bf16[1024,128]{1,0:T(8,128)(2,1)} %g_in.1, ...), custom_call_target="tpu_custom_call" | custom-call | tf_op jit(solution)/shard_map/pallas_call | solution.py:438
  46.1 1.7 %shard_map.95 = (bf16[1024,128]{1,0:T(8,128)(2,1)}, bf16[64,128]{1,0:T(8,128)(2,1)}, bf16[64,128]{1,0:T(8,128)(2,1)}) custom-call(bf16[1024,128]{1,0:T(8,128)(2,1)} %get-tuple-element.6.refs_0_, bf16[64,128]{1,0:T(8,128)(2,1)} %get-tuple-element.7.refs_1_, bf16[64,128]{1,0:T(8,128)(2,1)} %get-tuple-element.8.refs_2_), custom_call_target="tpu_custom_call" | custom-call | tf_op jit(solution)/shard_map/pallas_call | solution.py:489

commit v6 on v5

--- a/solution.py
+++ b/solution.py
@@ -197,6 +197,7 @@
     lead = max(steps - 1 - ahead, 0)
     loop(0, steps - 1 - lead, lambda i: when_sends(wave_v)(steps - 1 - i))
     down(when_has(spread_y))
+    down(when_has(features))
     await_bytes(rs_v, near_recv.at[0])
 
     v_lane = lax.broadcasted_iota(jnp.int32, (1, 128), 1)
@@ -250,9 +251,9 @@
 
         @pl.when(s > 1)
         def _():
-            loop(1, ys, lambda j: to_y(s, j).start())
             part_v[s] = acc[1].astype(BF16)
             v_to_owner(s).start()
+            loop(1, ys, lambda j: to_y(s, j).start())
 
     def sum_y(s):
         await_bytes(rs_k.at[s], r_p.at[s])
@@ -295,7 +296,6 @@
         return remote(sum_v.at[pz, py], rs_v.at[j - 1], last_send.at[1], last_recv.at[1], to)
 
     loop(1, half, lambda j: last_k(j).start())
-    down(when_has(features))
 
     def once(s, fn):
         if isinstance(s, int) and s >= steps:
@@ -350,10 +350,10 @@
     def far(fn):
         loop(0, steps - 2, lambda i: fn(steps - 1 - i))
 
-    once(3, sum_z)
     far(when_sends(collect_v))
     sum_v[...] = acc_own[1].astype(BF16).reshape(2, ys, own, hd)
     loop(1, half, lambda j: last_v(j).start())
+    once(3, sum_z)
     once(2, sum_z)
 
     sib_d.wait_recv()

time: 48 us -> 47.8 us (level)
  no operation moved by 1% of the time
where the time goes in v6:
time: 47.8 us; the launch traced here: 47.6 us
  Pallas kernels  47 us (98%)
  between operations  0.64 us (1%)
    pallas_call x1, Pallas kernels, body(): pl.pallas_call(functools.partial(kernel, n_ctx, n_tp, steps), out_shape=(...  45.3 us
    pallas_call x1, Pallas kernels, body(): pl.pallas_call(hand_over, out_shape=tuple((jax.ShapeDtypeStruct(x.shape,...  1.69 us

profile of v6, /device:TPU:4, one launch (start us, length us, event | category | flops | bytes accessed | tf_op | source)
XLA Modules:
  0.0 47.6 jit_solution(12560942348672196890)
XLA Ops:
  0.6 45.3 %shard_map.94 = (bf16[1024,128]{1,0:T(8,128)(2,1)}, bf16[64,128]{1,0:T(8,128)(2,1)}, bf16[64,128]{1,0:T(8,128)(2,1)}) custom-call(bf16[1024,128]{1,0:T(8,128)(2,1)} %q_in.1, bf16[64,128]{1,0:T(8,128)(2,1)} %k_in.1, bf16[64,128]{1,0:T(8,128)(2,1)} %v_in.1, bf16[1024,128]{1,0:T(8,128)(2,1)} %o_in.1, bf16[1024,128]{1,0:T(8,128)(2,1)} %g_in.1, ...), custom_call_target="tpu_custom_call" | custom-call | tf_op jit(solution)/shard_map/pallas_call | solution.py:438
  45.9 1.7 %shard_map.95 = (bf16[1024,128]{1,0:T(8,128)(2,1)}, bf16[64,128]{1,0:T(8,128)(2,1)}, bf16[64,128]{1,0:T(8,128)(2,1)}) custom-call(bf16[1024,128]{1,0:T(8,128)(2,1)} %get-tuple-element.6.refs_0_, bf16[64,128]{1,0:T(8,128)(2,1)} %get-tuple-element.7.refs_1_, bf16[64,128]{1,0:T(8,128)(2,1)} %get-tuple-element.8.refs_2_), custom_call_target="tpu_custom_call" | custom-call | tf_op jit(solution)/shard_map/pallas_call | solution.py:489

commit v7 on v6

--- a/solution.py
+++ b/solution.py
@@ -149,8 +149,7 @@
     extra = jnp.zeros((8, rows), F32)
     for i, row in enumerate((*split3(lse[...] * math.sqrt(hd)), *split3(delta))):
         extra = jnp.where(place == i, -row, extra)
-    xt[0, 0:8, :] = jnp.where(place == q_doc, -FAR, 0.0).astype(BF16)
-    xt[0, 8:16, :] = extra.astype(BF16)
+    xt[0, 0:16, :] = jnp.concatenate([jnp.where(place == q_doc, -FAR, 0.0), extra], axis=0).astype(BF16)
 
     sib_x.start()
 
@@ -420,9 +419,19 @@
 
 
 def hand_over(*refs):
-    half = len(refs) // 2
-    for src, dst in zip(refs[:half], refs[half:]):
-        dst[...] = src[...]
+    half = 3
+    src, dst, held, came, went = refs[:half], refs[half:2 * half], refs[2 * half:3 * half], refs[-2], refs[-1]
+    pieces = [(0, pl.ds(k * (src[0].shape[0] // 4), src[0].shape[0] // 4)) for k in range(4)]
+    pieces += [(i, pl.ds(0, src[i].shape[0])) for i in range(1, half)]
+    loads = [pltpu.make_async_copy(src[i].at[at], held[i].at[at], came.at[n]) for n, (i, at) in enumerate(pieces)]
+    stores = [pltpu.make_async_copy(held[i].at[at], dst[i].at[at], went.at[n]) for n, (i, at) in enumerate(pieces)]
+    for load in loads:
+        load.start()
+    for load, store in zip(loads, stores):
+        load.wait()
+        store.start()
+    for store in stores:
+        store.wait()
 
 
 def body(n_ctx, n_tp, queries, keys, values, outputs, out_grad, log_norm, doc_ids):
@@ -489,8 +498,10 @@
     return pl.pallas_call(
         hand_over,
         out_shape=tuple(jax.ShapeDtypeStruct(x.shape, x.dtype) for x in grads),
-        in_specs=[inside] * 3,
-        out_specs=(inside,) * 3,
+        in_specs=[anywhere] * 3,
+        out_specs=(anywhere,) * 3,
+        scratch_shapes=[*[pltpu.VMEM(x.shape, x.dtype) for x in grads], dma((6,)), dma((6,))],
+        compiler_params=pltpu.CompilerParams(vmem_limit_bytes=63 * 1024 * 1024),
     )(*grads)
 
 

time: 47.8 us -> 47.7 us (level)
  no operation moved by 1% of the time
where the time goes in v7:
time: 47.7 us; the launch traced here: 47.6 us
  Pallas kernels  46.9 us (98%)
  between operations  0.64 us (1%)
    pallas_call x1, Pallas kernels, body(): pl.pallas_call(functools.partial(kernel, n_ctx, n_tp, steps), out_shape=(...  45.3 us
    pallas_call x1, Pallas kernels, body(): pl.pallas_call(hand_over, out_shape=tuple((jax.ShapeDtypeStruct(x.shape,...  1.67 us

profile of v7, /device:TPU:4, one launch (start us, length us, event | category | flops | bytes accessed | tf_op | source)
XLA Modules:
  0.0 47.6 jit_solution(17304714216153837887)
XLA Ops:
  0.6 45.3 %shard_map.94 = (bf16[1024,128]{1,0:T(8,128)(2,1)}, bf16[64,128]{1,0:T(8,128)(2,1)}, bf16[64,128]{1,0:T(8,128)(2,1)}) custom-call(bf16[1024,128]{1,0:T(8,128)(2,1)} %q_in.1, bf16[64,128]{1,0:T(8,128)(2,1)} %k_in.1, bf16[64,128]{1,0:T(8,128)(2,1)} %v_in.1, bf16[1024,128]{1,0:T(8,128)(2,1)} %o_in.1, bf16[1024,128]{1,0:T(8,128)(2,1)} %g_in.1, ...), custom_call_target="tpu_custom_call" | custom-call | tf_op jit(solution)/shard_map/pallas_call | solution.py:447
  45.9 1.7 %shard_map.95 = (bf16[1024,128]{1,0:T(8,128)(2,1)}, bf16[64,128]{1,0:T(8,128)(2,1)}, bf16[64,128]{1,0:T(8,128)(2,1)}) custom-call(bf16[1024,128]{1,0:T(8,128)(2,1)} %get-tuple-element.6.refs_0_, bf16[64,128]{1,0:T(8,128)(2,1)} %get-tuple-element.7.refs_1_, bf16[64,128]{1,0:T(8,128)(2,1)} %get-tuple-element.8.refs_2_), custom_call_target="tpu_custom_call" | custom-call | tf_op jit(solution)/shard_map/pallas_call | solution.py:498

commit v8 on v7

--- a/solution.py
+++ b/solution.py
@@ -59,9 +59,6 @@
             (o_in, on), (lse_in, lse), (doc_in, doc),
         ))
     ]
-    for load in loads:
-        load.start()
-
     def loop(first, last, fn):
         def one(i, _):
             fn(i)
@@ -104,9 +101,13 @@
     def greet(to):
         pl.semaphore_signal(barrier, inc=1, device_id=to, device_id_type=MESH)
 
-    greet(sib)
+    for load in loads[:2]:
+        load.start()
     loop(1, half, lambda j: greet(peer(j)[2]))
     loop(1, n_ctx, lambda j: greet(((c + j) % n_ctx, t)))
+    greet(sib)
+    for load in loads[2:]:
+        load.start()
 
     def near_k(j):
         return remote(kb.at[0, z, y], kb.at[0, z, y], near_send.at[0], near_recv.at[0], peer(j)[2])

time: 47.7 us -> 47.7 us (level)
  no operation moved by 1% of the time
where the time goes in v8:
time: 47.7 us; the launch traced here: 47.5 us
  Pallas kernels  46.9 us (98%)
  between operations  0.64 us (1%)
    pallas_call x1, Pallas kernels, body(): pl.pallas_call(functools.partial(kernel, n_ctx, n_tp, steps), out_shape=(...  45.2 us
    pallas_call x1, Pallas kernels, body(): pl.pallas_call(hand_over, out_shape=tuple((jax.ShapeDtypeStruct(x.shape,...  1.67 us

profile of v8, /device:TPU:4, one launch (start us, length us, event | category | flops | bytes accessed | tf_op | source)
XLA Modules:
  0.0 47.5 jit_solution(4510666367469198912)
XLA Ops:
  0.6 45.2 %shard_map.94 = (bf16[1024,128]{1,0:T(8,128)(2,1)}, bf16[64,128]{1,0:T(8,128)(2,1)}, bf16[64,128]{1,0:T(8,128)(2,1)}) custom-call(bf16[1024,128]{1,0:T(8,128)(2,1)} %q_in.1, bf16[64,128]{1,0:T(8,128)(2,1)} %k_in.1, bf16[64,128]{1,0:T(8,128)(2,1)} %v_in.1, bf16[1024,128]{1,0:T(8,128)(2,1)} %o_in.1, bf16[1024,128]{1,0:T(8,128)(2,1)} %g_in.1, ...), custom_call_target="tpu_custom_call" | custom-call | tf_op jit(solution)/shard_map/pallas_call | solution.py:448
  45.8 1.7 %shard_map.95 = (bf16[1024,128]{1,0:T(8,128)(2,1)}, bf16[64,128]{1,0:T(8,128)(2,1)}, bf16[64,128]{1,0:T(8,128)(2,1)}) custom-call(bf16[1024,128]{1,0:T(8,128)(2,1)} %get-tuple-element.6.refs_0_, bf16[64,128]{1,0:T(8,128)(2,1)} %get-tuple-element.7.refs_1_, bf16[64,128]{1,0:T(8,128)(2,1)} %get-tuple-element.8.refs_2_), custom_call_target="tpu_custom_call" | custom-call | tf_op jit(solution)/shard_map/pallas_call | solution.py:499
